TPU v7x, 128 devices: a whole 4x4x4 slice. The times are simulated.
128 devices in a mesh: dom: 16 (over z, x), grp: 8 (over y, core).
Axes of the slice: x: 4, y: 4, z: 4, core: 2. Of those that a mesh axis runs over, the one named last changes fastest.
Arguments:
- nodes: bfloat16 [131072, 256], P(('dom', 'grp')), may hold values from -6 to 6
- edges: bfloat16 [524288, 256], P(('dom', 'grp')), may hold values from -6 to 6
- senders: int32 [524288], P(('dom', 'grp')), may hold values from 0 to 1535, as said below
- receivers: int32 [524288], P(('dom', 'grp')), may hold values from 0 to 1023, as said below
- edge_count: int32 [128], P(('dom', 'grp')), may hold values from 64 to 512, as said below
- halo_rows: int32 [128, 16, 32], P(('dom', 'grp')), may hold values from 0 to 1023, as said below
- aggregates: int32 [131072], P(('dom', 'grp')), may hold values from 0 to 1023, as said below
- coarse_edges: bfloat16 [16, 4096, 256], P('dom'), may hold values from -6 to 6
- coarse_senders: int32 [16, 4096], P('dom'), may hold values from 0 to 1023
- coarse_receivers: int32 [16, 4096], P('dom'), may hold values from 0 to 127
- cotangent: bfloat16 [131072, 256], P(('dom', 'grp')), may hold values from -6 to 6
- fine_weights: bfloat16 [1792, 256], replicated, may hold values from -0.21875 to 0.21875
- coarse_weights: bfloat16 [1792, 256], replicated, may hold values from -0.21875 to 0.21875
Outputs:
- fine_out: bfloat16 [131072, 256], P(('dom', 'grp'))
- node_grad: bfloat16 [131072, 256], P(('dom', 'grp'))
- edge_grad: bfloat16 [524288, 256], P(('dom', 'grp'))
- fine_weight_grad: float32 [1792, 256], replicated
- coarse_weight_grad: float32 [1792, 256], replicated
Inputs may be any that keep to these rules, and one draw needn't show every extreme that they name: `senders`: A value at least 1024 names a halo slot from a partition at another dom index with the same grp index. The receivers of edge slots 512 * t to 512 * t + 511 of a partition lie in its node rows 128 * t to 128 * t + 127. `edge_count`: each count is 512 divided by a power of two; some partition has 512 and some 64. `halo_rows`: entry [q, p, t] is a local node row of partition q; the rows of one list are distinct. `aggregates`: every coarse node of a group is the aggregate of exactly 8 fine nodes of that group.
All inputs are finite; a program needn't handle non-finite values.
Results may differ from a plain program's by a relative error of at most 0.035.
Values may be sent and summed in bfloat16 or wider, within the bound.
A program may use at most 128 MiB of HBM per device.

v0:
```python
import jax
import jax.numpy as jnp
from jax import lax
from jax.sharding import PartitionSpec as P


def stored(values):
    return lax.optimization_barrier(values.astype(jnp.bfloat16))


def layer_norm(values):
    centre = values - jnp.mean(values, axis=-1, keepdims=True)
    spread = jnp.mean(centre * centre, axis=-1, keepdims=True)
    return centre * lax.rsqrt(spread + 1e-05)


def two_layer(inputs, first, second):
    hidden = jnp.dot(inputs, first, preferred_element_type=jnp.float32)
    active = jax.nn.silu(hidden).astype(jnp.bfloat16)
    return layer_norm(jnp.dot(active, second, preferred_element_type=jnp.float32))


def edge_message(edge_rows, sender_rows, target_rows, weights):
    feat_width = edge_rows.shape[1]
    narrow = weights.astype(jnp.bfloat16)
    joined = jnp.concatenate([edge_rows, sender_rows, target_rows], axis=1)
    return stored(
        two_layer(joined, narrow[: 3 * feat_width], narrow[3 * feat_width : 4 * feat_width])
    )


def node_update(node_rows, summed, weights):
    feat_width = node_rows.shape[1]
    narrow = weights.astype(jnp.bfloat16)
    joined = jnp.concatenate([node_rows, summed], axis=1)
    change = two_layer(joined, narrow[4 * feat_width : 6 * feat_width], narrow[6 * feat_width :])
    return stored(node_rows.astype(jnp.float32) + change)


def tile_sum(messages, receivers, live_mask, node_count):
    tile_rows = 128
    tile_count = node_count // tile_rows
    per_tile = messages.shape[0] // tile_count
    offsets = (
        receivers.reshape(tile_count, per_tile)
        - tile_rows * jnp.arange(tile_count, dtype=jnp.int32)[:, None]
    )
    onehot = (
        (offsets[:, :, None] == jnp.arange(tile_rows, dtype=jnp.int32)[None, None, :])
        & live_mask.reshape(tile_count, per_tile)[:, :, None]
    ).astype(jnp.bfloat16)
    summed = jnp.einsum(
        "tek,teh->tkh",
        onehot,
        messages.reshape(tile_count, per_tile, -1),
        preferred_element_type=jnp.float32,
    )
    return summed.reshape(node_count, -1).astype(jnp.bfloat16)


def block_sum(messages, receivers, blocks, own_rows):
    onehot = (
        receivers.reshape(blocks, -1)[:, :, None]
        == jnp.arange(own_rows, dtype=jnp.int32)[None, None, :]
    ).astype(jnp.bfloat16)
    summed = jnp.einsum(
        "bek,beh->bkh",
        onehot,
        messages.reshape(blocks, onehot.shape[1], -1),
        preferred_element_type=jnp.float32,
    )
    return summed.reshape(blocks * own_rows, -1).astype(jnp.bfloat16)


def coarse_layer(source_rows, edge_rows, send_rows, recv_rows, blocks, own_rows, weights):
    local_index = (
        jnp.arange(blocks, dtype=jnp.int32)[:, None] * own_rows + recv_rows.reshape(blocks, -1)
    ).reshape(-1)
    sender_rows = jnp.take(source_rows, send_rows, axis=0).astype(jnp.bfloat16)
    target_rows = jnp.take(source_rows, local_index, axis=0).astype(jnp.bfloat16)
    messages = edge_message(edge_rows, sender_rows, target_rows, weights)
    return node_update(
        source_rows.astype(jnp.bfloat16), block_sum(messages, recv_rows, blocks, own_rows), weights
    )


def body(
    nodes,
    edges,
    senders,
    receivers,
    edge_count,
    halo_rows,
    aggregates,
    coarse_edges,
    coarse_senders,
    coarse_receivers,
    cotangent,
    fine_weights,
    coarse_weights,
):
    node_count, feat_width = nodes.shape
    groups = lax.axis_size("grp")
    domains = lax.axis_size("dom")
    own_rows = node_count // 8
    group_rows = own_rows * groups
    slot_count = halo_rows.shape[2]
    per_block = coarse_senders.shape[1] // groups
    fine_float = fine_weights.astype(jnp.float32)
    coarse_float = coarse_weights.astype(jnp.float32)
    positions = jnp.arange(edges.shape[0], dtype=jnp.int32)
    live_mask = positions % 512 < edge_count[0]
    send_index = halo_rows[0].reshape(-1)
    outgoing = jnp.take(nodes, send_index, axis=0).reshape(domains, slot_count, feat_width)
    incoming = lax.all_to_all(outgoing, "dom", split_axis=0, concat_axis=0, tiled=True)
    sources = jnp.concatenate(
        [nodes, incoming.reshape(domains * slot_count, feat_width)], axis=0
    ).astype(jnp.float32)

    def fine_part(source_rows, edge_rows, weights):
        node_wide = source_rows[:node_count]
        sender_rows = jnp.take(source_rows, senders, axis=0).astype(jnp.bfloat16)
        target_rows = jnp.take(node_wide, receivers, axis=0).astype(jnp.bfloat16)
        messages = edge_message(edge_rows, sender_rows, target_rows, weights)
        summed = tile_sum(messages, receivers, live_mask, node_count)
        return node_update(node_wide.astype(jnp.bfloat16), summed, weights)

    refined, fine_back = jax.vjp(fine_part, sources, edges, fine_float)
    member = (aggregates[:, None] == jnp.arange(group_rows, dtype=jnp.int32)[None, :]).astype(
        jnp.bfloat16
    )
    contract = (((0,), (0,)), ((), ()))

    def group_total(values):
        return lax.psum(values.astype(jnp.bfloat16), "grp").astype(jnp.float32)

    partial_value = (
        lax.dot_general(member, refined, contract, preferred_element_type=jnp.float32) * 0.125
    )
    coarse_input = stored(group_total(partial_value))

    def coarse_part(source_rows, weights):
        return coarse_layer(
            source_rows,
            coarse_edges[0],
            coarse_senders[0],
            coarse_receivers[0],
            groups,
            own_rows,
            weights,
        )

    coarse_table, coarse_back = jax.vjp(coarse_part, coarse_input.astype(jnp.float32), coarse_float)
    prolong_grad = group_total(
        lax.dot_general(member, cotangent, contract, preferred_element_type=jnp.float32)
    ).astype(jnp.bfloat16)
    source_grad, coarse_grad = coarse_back(prolong_grad)
    restrict_grad = (
        jnp.dot(member, source_grad.astype(jnp.bfloat16), preferred_element_type=jnp.float32)
        * 0.125
    )
    lifted = jnp.dot(member, coarse_table, preferred_element_type=jnp.float32)
    fine_out = (refined.astype(jnp.float32) + lifted).astype(jnp.bfloat16)
    refined_grad = (cotangent.astype(jnp.float32) + restrict_grad).astype(jnp.bfloat16)
    source_rows_grad, edge_grad, fine_grad = fine_back(refined_grad)
    returned = lax.all_to_all(
        source_rows_grad[node_count:].reshape(domains, slot_count, feat_width).astype(jnp.bfloat16),
        "dom",
        split_axis=0,
        concat_axis=0,
        tiled=True,
    ).astype(jnp.float32)
    node_grad = (
        source_rows_grad[:node_count]
        .at[send_index]
        .add(returned.reshape(-1, feat_width))
        .astype(jnp.bfloat16)
    )
    fine_scale = (edges.shape[0] * domains * groups) ** (-0.5)
    coarse_scale = (per_block * groups * domains) ** (-0.5)
    fine_total = lax.psum(fine_grad, ("dom", "grp"))
    coarse_total = lax.psum(coarse_grad.astype(jnp.bfloat16), "dom").astype(jnp.float32)
    return (fine_out, node_grad, edge_grad, fine_total * fine_scale, coarse_total * coarse_scale)


def solution(mesh):
    placed = (
        P(("dom", "grp"), None),
        P(("dom", "grp"), None),
        P(("dom", "grp")),
        P(("dom", "grp")),
        P(("dom", "grp")),
        P(("dom", "grp"), None, None),
        P(("dom", "grp")),
        P("dom", None, None),
        P("dom", None),
        P("dom", None),
        P(("dom", "grp"), None),
        P(),
        P(),
    )
    return jax.shard_map(
        body,
        mesh=mesh,
        in_specs=placed,
        out_specs=(
            P(("dom", "grp"), None),
            P(("dom", "grp"), None),
            P(("dom", "grp"), None),
            P(),
            P(),
        ),
        check_vma=False,
    )
```

profile of v0, /device:TPU:1, one launch (start us, length us, event | category | flops | bytes accessed | tf_op | source)
XLA Modules:
  0.0 562.9 jit_solution(14931250614218260820)
XLA Ops:
  8.8 2.7 gather_fusion
  12.3 8.4 %all-to-all-start = ((bf16[16,32,256]{2,1,0:T(8,128)(2,1)}), bf16[16,32,256]{2,1,0:T(8,128)(2,1)S(1)}, u32[]{:S(2)}, u32[]{:S(2)}) async-start(bf16[16,32,256]{2,1,0:T(8,128)(2,1)} %broadcast_select_fusion), calls=%async_computation | async-start | bytes 524288 | tf_op jit(solution)/shard_map/all_to_all | solution.py:115
  29.4 1.9 fusion.61
  32.1 17.0 %gather_fusion.1 = bf16[4096,256]{1,0:T(8,128)(2,1)} fusion(bf16[1536,256]{1,0:T(8,128)(2,1)S(1)} %copy.48, s32[4096]{0:T(1024)S(1)} %get-tuple-element.42), kind=kCustom, calls=%fused_computation.4 | custom fusion | bytes 4210688 | tf_op jit(solution)/shard_map/jvp(jit(_take))/gather | solution.py:122
  49.0 17.0 %gather_fusion.2 = bf16[4096,256]{1,0:T(8,128)(2,1)} fusion(bf16[1024,256]{1,0:T(8,128)(2,1)S(1)} %copy.49, s32[4096]{0:T(1024)S(1)} %get-tuple-element.44), kind=kCustom, calls=%fused_computation.clone | custom fusion | bytes 4210688 | tf_op jit(solution)/shard_map/jvp(jit(_take))/gather | solution.py:123
  66.1 5.3 select_convert_fusion.2
  71.4 1.8 fusion.27
  78.0 1.8 multiply_convert_fusion.2
  79.8 4.1 copy.80
  83.9 3.3 fusion.55
  90.3 1.8 fusion.60
  95.1 59.9 %all-reduce.18.cloned.1.call-done = (bf16[1024,256]{0,1:T(8,128)(2,1)}, bf16[1024,256]{0,1:T(8,128)(2,1)}) async-done(((bf16[1024,256]{0,1:T(8,128)(2,1)}, bf16[1024,256]{0,1:T(8,128)(2,1)}), (bf16[1024,256]{0,1:T(8,128)(2,1)}, bf16[1024,256]{0,1:T(8,128)(2,1)})) %all-reduce.18.cloned.1.call-update) | async-done | bytes 1048592 | tf_op jit(solution)/shard_map/psum | solution.py:135
  156.2 17.3 %gather_fusion.4 = bf16[4096,256]{1,0:T(8,128)(2,1)} fusion(bf16[1024,256]{1,0:T(8,128)(2,1)S(1)} %copy.54, s32[4096]{0:T(1024)S(1)} %broadcast_clamp_fusion), kind=kCustom, calls=%fused_computation.2.clone | custom fusion | bytes 4210688 | tf_op jit(solution)/shard_map/jvp(jit(_take))/gather | solution.py:80
  173.4 16.9 %gather_fusion.3 = bf16[4096,256]{1,0:T(8,128)(2,1)} fusion(bf16[1024,256]{1,0:T(8,128)(2,1)S(1)} %copy.54, s32[4096]{0:T(1024)S(1)} %get-tuple-element.46), kind=kCustom, calls=%fused_computation.1.clone | custom fusion | bytes 4210688 | tf_op jit(solution)/shard_map/jvp(jit(_take))/gather | solution.py:79
  190.4 2.1 select_convert_fusion
  192.6 2.1 select_convert_fusion.1
  194.8 1.8 fusion.25
  201.1 2.5 copy.81
  203.5 3.0 fusion.62
  214.7 2.4 fusion.50
  217.1 2.9 copy.84
  220.0 3.0 fusion
  225.3 3.0 fusion.65
  228.3 4.9 fusion.1
  234.7 6.1 %convolution_convert_fusion.1 = bf16[4096,768]{1,0:T(8,128)(2,1)} fusion(bf16[4096,256]{1,0:T(8,128)(2,1)} %fusion.1, bf16[1792,256]{1,0:T(8,128)(2,1)} %param.27), kind=kOutput, calls=%fused_computation.11 | convolution fusion | flops 1610612736 | bytes 8781824 | tf_op jit(solution)/shard_map/transpose(jvp())/dot_general | solution.py:18
  240.8 23.4 %scatter_custom_fusion = f32[1024,256]{1,0:T(8,128)S(1)} fusion(f32[1024,256]{1,0:T(8,128)S(1)} %copy.65, s32[4096]{0:T(1024)S(1)} %copy-done.40, bf16[4096,768]{1,0:T(8,128)(2,1)} %convolution_convert_fusion.1), kind=kCustom, calls=%fused_computation.43 | custom fusion | flops 2097152 | bytes 3145728 | tf_op jit(solution)/shard_map/transpose(jvp(jit(_take)))/scatter-add | solution.py:80
  264.3 21.3 %scatter_custom_fusion.1 = f32[1024,256]{1,0:T(8,128)S(1)} fusion(s32[4096]{0:T(1024)} %get-tuple-element.45, bf16[4096,768]{1,0:T(8,128)(2,1)} %convolution_convert_fusion.1, f32[]{:T(128)} %constant.100.clone.1), kind=kCustom, calls=%fused_computation.41 | custom fusion | flops 2097152 | bytes 3146240 | tf_op jit(solution)/shard_map/transpose(jvp(jit(_take)))/scatter-add | solution.py:79
  285.6 2.3 fusion.58
  289.7 1.7 fusion.75
  294.4 3.2 fusion.47
  297.7 2.9 copy.86
  300.6 3.0 fusion.3
  305.9 2.3 fusion.68
  308.2 4.1 fusion.4
  312.3 1.8 fusion.63
  316.5 4.2 fusion.64
  322.6 5.5 convolution_convert_fusion
  329.4 3.1 split.44
  332.5 25.2 %scatter_custom_fusion.2 = f32[1024,256]{1,0:T(8,128)} fusion(f32[1024,256]{1,0:T(8,128)} %copy.70, s32[4096]{0:T(1024)} %get-tuple-element.43, bf16[4096,768]{1,0:T(8,128)(2,1)} %convolution_convert_fusion), kind=kCustom, calls=%fused_computation.39 | custom fusion | flops 2097152 | bytes 3145728 | tf_op jit(solution)/shard_map/transpose(jvp(jit(_take)))/scatter-add | solution.py:123
  359.0 23.6 %scatter_custom_fusion.3 = f32[1536,256]{1,0:T(8,128)S(1)} fusion(f32[1536,256]{1,0:T(8,128)S(1)} %pad.27, s32[4096]{0:T(1024)} %get-tuple-element.41, bf16[4096,768]{1,0:T(8,128)(2,1)} %convolution_convert_fusion), kind=kCustom, calls=%fused_computation.37 | custom fusion | flops 2097152 | bytes 3670016 | tf_op jit(solution)/shard_map/transpose(jvp(jit(_take)))/scatter-add | solution.py:122
  383.5 6.7 %all-to-all-start.1 = ((bf16[16,32,256]{2,1,0:T(8,128)(2,1)}), bf16[16,32,256]{2,1,0:T(8,128)(2,1)S(1)}, u32[]{:S(2)}, u32[]{:S(2)}) async-start(bf16[16,32,256]{2,1,0:T(8,128)(2,1)} %bitcast.19), calls=%async_computation.1 | async-start | bytes 524288 | tf_op jit(solution)/shard_map/all_to_all | solution.py:166
  390.2 2.2 fusion.59
  393.4 4.3 all-to-all-done.1
  397.7 3.9 scatter_custom_fusion.4
  402.4 64.8 %all-reduce.14.cloned.1.call-done = f32[1792,256]{1,0:T(8,128)} async-done(((f32[1792,256]{1,0:T(8,128)}), f32[1792,256]{1,0:T(8,128)}) %all-reduce.14.cloned.1.call-update) | async-done | bytes 1835024 | tf_op jit(solution)/shard_map/psum | solution.py:181
  467.3 2.9 broadcast_multiply_fusion
  470.1 83.3 %all-reduce.16.cloned.1.call-done = bf16[1792,256]{1,0:T(8,128)(2,1)} async-done(((bf16[1792,256]{1,0:T(8,128)(2,1)}), bf16[1792,256]{1,0:T(8,128)(2,1)}) %all-reduce.16.cloned.1.call-update) | async-done | bytes 917520 | tf_op jit(solution)/shard_map/psum | solution.py:182
  553.4 2.5 convert_multiply_fusion.8
  (206 shorter events, 56.0 us)
Async XLA Ops:
  7.2 21.6 %copy-start.38 = (s32[1,4096]{1,0:T(1,128)S(1)}, s32[1,4096]{1,0:T(1,128)}, u32[]{:S(2)}) copy-start(s32[1,4096]{1,0:T(1,128)} %param.24) | copy-start | bytes 49156
  7.2 22.2 %copy-start.48 = (s32[1024]{0:T(1024)S(1)}, s32[1024]{0:T(1024)}, u32[]{:S(2)}) copy-start(s32[1024]{0:T(1024)} %param.21) | copy-start | bytes 12292
  7.2 22.2 %copy-start.19 = (bf16[1024,256]{1,0:T(8,128)(2,1)S(1)}, bf16[1024,256]{1,0:T(8,128)(2,1)}, u32[]{:S(2)}) copy-start(bf16[1024,256]{1,0:T(8,128)(2,1)} %param.25) | copy-start | bytes 1572868
  8.7 12.0 %copy-start.44 = (s32[512,1]{0,1:T(1,128)}, s32[512,1]{0,1:T(1,128)S(1)}, u32[]{:S(2)}) copy-start(s32[512,1]{0,1:T(1,128)S(1)} %compare_select_fusion.5) | copy-start | bytes 6148
  12.3 19.0 %all-to-all-start = ((bf16[16,32,256]{2,1,0:T(8,128)(2,1)}), bf16[16,32,256]{2,1,0:T(8,128)(2,1)S(1)}, u32[]{:S(2)}, u32[]{:S(2)}) async-start(bf16[16,32,256]{2,1,0:T(8,128)(2,1)} %broadcast_select_fusion), calls=%async_computation | async-start | bytes 524288 | tf_op jit(solution)/shard_map/all_to_all | solution.py:115
  20.7 134.2 %all-reduce.18.cloned.1.call-start = ((), (), s32[]{:S(2)}) async-start(), calls=%async_computation.4 | async-start | bytes 2097152 | tf_op jit(solution)/shard_map/psum | solution.py:135
  31.6 55.8 %copy-start.16 = (bf16[1024,256]{0,1:T(8,128)(2,1)}, bf16[1024,256]{0,1:T(8,128)(2,1)S(1)}, u32[]{:S(2)}) copy-start(bf16[1024,256]{0,1:T(8,128)(2,1)S(1)} %slice.106) | copy-start | bytes 1572868
  66.1 5.3 copy-start.26
  66.1 5.3 copy-start.45
  73.4 2.0 copy-start.54
  75.4 2.1 copy-start
  78.0 5.9 %copy-start.35 = (s32[8,512]{1,0:T(8,128)S(1)}, s32[8,512]{1,0:T(8,128)}, u32[]{:S(2)}) copy-start(s32[8,512]{1,0:T(8,128)} %get-tuple-element.50) | copy-start | bytes 49156
  78.0 5.9 %copy-start.41 = (pred[8,512]{1,0:T(8,128)(4,1)S(1)}, pred[8,512]{1,0:T(8,128)(4,1)}, u32[]{:S(2)}) copy-start(pred[8,512]{1,0:T(8,128)(4,1)} %fusion.119) | copy-start | bytes 12292
  89.9 2.3 copy-start.37
  89.9 2.3 copy-start.20
  89.9 3.8 copy-start.39
  89.9 4.5 copy-start.40
  90.3 83.2 %copy-start.23 = (bf16[1024,256]{0,1:T(8,128)(2,1)}, bf16[1024,256]{0,1:T(8,128)(2,1)S(1)}, u32[]{:S(2)}) copy-start(bf16[1024,256]{0,1:T(8,128)(2,1)S(1)} %add_convert_fusion.3) | copy-start | bytes 1572868
  92.1 375.1 %all-reduce.14.cloned.1.call-start = ((), (), s32[]{:S(2)}) async-start(), calls=%async_computation.2 | async-start | bytes 3670016 | tf_op jit(solution)/shard_map/psum | solution.py:181
  173.4 17.0 %copy-start.43 = (pred[4096]{0:T(1024)(128)(4,1)S(1)}, pred[4096]{0:T(1024)(128)(4,1)}, u32[]{:S(2)}) copy-start(pred[4096]{0:T(1024)(128)(4,1)} %get-tuple-element.31) | copy-start | bytes 12292
  190.4 2.2 copy-start.4
  190.4 4.4 copy-start.24
  190.4 4.4 copy-start.47
  192.6 4.0 copy-start.13
  198.6 2.0 copy-start.2
  203.5 4.9 copy-start.25
  206.7 2.2 copy-start.5
  206.8 2.5 copy-start.15
  220.0 3.5 copy-start.3
  223.0 2.3 copy-start.57
  240.8 44.8 %copy-start.50 = (s32[1024]{0:T(1024)S(1)}, s32[1024]{0:T(1024)}, u32[]{:S(2)}) copy-start(s32[1024]{0:T(1024)} %param.21) | copy-start | bytes 12292
  285.6 2.8 copy-start.53
  291.5 2.9 copy-start.36
  291.5 2.9 copy-start.42
  300.6 3.0 copy-start.31
  300.6 3.5 copy-start.1
  300.6 3.4 copy-start.29
  303.6 2.3 copy-start.55
  308.2 4.1 copy-start.10
  308.2 4.1 copy-start.12
  308.2 4.1 copy-start.46
  314.2 2.3 copy-start.6
  315.6 5.0 copy-start.32
  315.6 237.8 %all-reduce.16.cloned.1.call-start = ((), (), s32[]{:S(2)}) async-start(), calls=%async_computation.3 | async-start | bytes 1835008 | tf_op jit(solution)/shard_map/psum | solution.py:182
  316.5 4.2 copy-start.33
  357.6 32.5 %copy-start.18 = (bf16[1024,256]{0,1:T(8,128)(2,1)S(1)}, bf16[1024,256]{0,1:T(8,128)(2,1)}, u32[]{:S(2)}) copy-start(bf16[1024,256]{0,1:T(8,128)(2,1)} %get-tuple-element.34) | copy-start | bytes 1572868
  357.6 32.5 %copy-start.51 = (s32[1024]{0:T(1024)S(1)}, s32[1024]{0:T(1024)}, u32[]{:S(2)}) copy-start(s32[1024]{0:T(1024)} %param.21) | copy-start | bytes 12292
  383.5 14.2 %all-to-all-start.1 = ((bf16[16,32,256]{2,1,0:T(8,128)(2,1)}), bf16[16,32,256]{2,1,0:T(8,128)(2,1)S(1)}, u32[]{:S(2)}, u32[]{:S(2)}) async-start(bf16[16,32,256]{2,1,0:T(8,128)(2,1)} %bitcast.19), calls=%async_computation.1 | async-start | bytes 524288 | tf_op jit(solution)/shard_map/all_to_all | solution.py:166
  (15 other events, 24.9 us)
Sparse Core Ops, SparseCore 0:
  92.2 62.6 all-reduce.17
  315.7 151.4 all-reduce.13
  470.6 82.7 all-reduce.15
where the time goes:
time: 574 us; the launch traced here: 563 us
  waiting for transfers between devices  212 us (37%)
  other arithmetic  139 us (24%)
  local copies, waits for them, and re-layouts  109 us (19%)
  matrix products  71.3 us (12%)
  between operations  15.9 us (3%)
  starting transfers between devices  15.2 us (3%)
    psum x1, waiting for transfers between devices, body(): lax.psum(coarse_grad.astype(jnp.bfloat16), 'dom').astype(jnp.float32)  83.3 us
    psum x1, waiting for transfers between devices, body(): fine_total = lax.psum(fine_grad, ('dom', 'grp'))  64.8 us
    psum x1, waiting for transfers between devices, group_total(): return lax.psum(values.astype(jnp.bfloat16), 'grp').astype(jnp.float32)  59.9 us
    dot_general x12, matrix products, two_layer(): hidden = jnp.dot(inputs, first, preferred_element_type=jnp.float32)  26.8 us
    scatter-add x1, other arithmetic, fine_part(): target_rows = jnp.take(node_wide, receivers, axis=0).astype(jnp.bfloat16)  25.2 us
    dot_general x12, matrix products, two_layer(): jnp.dot(active, second, preferred_element_type=jnp.float32)  24.4 us
    scatter-add x1, other arithmetic, fine_part(): sender_rows = jnp.take(source_rows, senders, axis=0).astype(jnp.bfloat16)  23.6 us
    scatter-add x1, other arithmetic, coarse_layer(): jnp.take(source_rows, local_index, axis=0).astype(jnp.bfloat16)  23.4 us
  transfers between devices with their start and end apart: 5, of which 4 were waited for; matrix products, arithmetic and copies ran while one was open for 16% of the time, Pallas kernels for 0%

commit v1 on v0

v1 whole, which is shorter than its diff:
```python
import jax
import jax.numpy as jnp
from jax import lax
from jax.experimental import pallas as pl
from jax.experimental.pallas import tpu as pltpu
from jax.sharding import PartitionSpec as P

MESH = pl.DeviceIdType.MESH
BF = jnp.bfloat16
F32 = jnp.float32
W = 256
DOM = 16
GRP = 8
TILES = 8
FINE_SCALE = 524288 ** (-0.5)
COARSE_SCALE = 65536 ** (-0.5)


def mm(a, b):
    return jnp.dot(a, b, preferred_element_type=F32)


def mm_nt(a, b):
    return lax.dot_general(a, b, (((1,), (1,)), ((), ())), preferred_element_type=F32)


def mm_tn(a, b):
    return lax.dot_general(a, b, (((0,), (0,)), ((), ())), preferred_element_type=F32)


def iota(shape, axis):
    return lax.broadcasted_iota(jnp.int32, shape, axis)


def hot(mask):
    return jnp.where(mask, 1.0, 0.0).astype(BF)


def column(row):
    return jnp.broadcast_to(row, (128, 128)).T


def silu_parts(h):
    sig = 1.0 / (1.0 + jnp.exp(-h))
    active = h * sig
    return active.astype(BF), (sig * (1.0 + h - active)).astype(BF)


def norm(z):
    centre = z - jnp.mean(z, axis=-1, keepdims=True)
    rs = lax.rsqrt(jnp.mean(centre * centre, axis=-1, keepdims=True) + 1e-05)
    return centre * rs, rs


def norm_back(dy, y, rs):
    first = jnp.mean(dy, axis=-1, keepdims=True)
    second = jnp.mean(dy * y, axis=-1, keepdims=True)
    return (rs * (dy - first - y * second)).astype(BF)


class Exchange:
    def __init__(self, axis, count, me, src, dst, ssem, rsem, off):
        self.axis, self.count, self.me = axis, count, me
        self.src, self.dst, self.ssem, self.rsem, self.off = src, dst, ssem, rsem, off

    def copy(self, k):
        peer = lax.rem(self.me + k, self.count)
        return pltpu.make_async_remote_copy(
            src_ref=self.src(peer),
            dst_ref=self.dst(k),
            send_sem=self.ssem.at[self.off + k],
            recv_sem=self.rsem.at[self.off + k],
            device_id={self.axis: peer},
            device_id_type=MESH,
        )

    def each(self, act):
        def step(k, carry):
            act(self.copy(k))
            return carry

        lax.fori_loop(1, self.count, step, 0)

    def start(self):
        self.each(lambda c: c.start())

    def wait_recv(self):
        self.each(lambda c: c.wait_recv())

    def wait_send(self):
        self.each(lambda c: c.wait_send())


def summed_blocks(own, received, count):
    total = own.astype(F32)
    for k in range(1, count):
        total = total + received[k].astype(F32)
    return total


class AllReduce:
    def __init__(self, refs, d, g, ssem, rsem):
        (self.sa, self.ra, self.ta, self.ua, self.va, self.oa,
         self.sb, self.rb, self.tb, self.ub, self.vb, self.ob) = refs
        self.d, self.g = d, g
        mk = lambda axis, src, dst, off: Exchange(
            axis, DOM if axis == "dom" else GRP, d if axis == "dom" else g, src, dst, ssem, rsem, off)
        sa, ra, ta, ua, va, oa = self.sa, self.ra, self.ta, self.ua, self.va, self.oa
        sb, rb, tb, ub, vb, ob = self.sb, self.rb, self.tb, self.ub, self.vb, self.ob
        self.a1 = mk("grp", lambda p: sa.at[p], lambda k: ra.at[k], 0)
        self.b1 = mk("dom", lambda p: sb.at[p], lambda k: rb.at[k], 8)
        self.a2 = mk("dom", lambda p: ta.at[p], lambda k: ua.at[k], 24)
        self.b2 = mk("grp", lambda p: tb.at[p], lambda k: ub.at[k], 40)
        self.a3 = mk("dom", lambda p: va.at[d], lambda k: va.at[d], 48)
        self.b3 = mk("grp", lambda p: vb.at[g], lambda k: vb.at[g], 64)
        self.a4 = mk("grp", lambda p: oa.at[g], lambda k: oa.at[g], 72)
        self.b4 = mk("dom", lambda p: ob.at[d], lambda k: ob.at[d], 80)

    def stage1(self):
        self.b1.start()
        self.a1.start()

    def stage2(self):
        self.a1.wait_recv()
        total = summed_blocks(self.sa[self.g], self.ra, GRP)
        step = total.shape[0] // 8
        for p in range(DOM):
            i, j = p // 2, p % 2
            self.ta[p] = total[i * step:(i + 1) * step, j * 128:(j + 1) * 128]
        self.a2.start()
        self.b1.wait_recv()
        total = summed_blocks(self.sb[self.d], self.rb, DOM)
        step = total.shape[0] // 4
        for p in range(GRP):
            i, j = p // 2, p % 2
            self.tb[p] = total[i * step:(i + 1) * step, j * 128:(j + 1) * 128]
        self.b2.start()

    def stage3(self):
        self.a2.wait_recv()
        self.va[self.d] = summed_blocks(self.ta[self.d], self.ua, DOM)
        self.a3.start()
        self.b2.wait_recv()
        self.vb[self.g] = summed_blocks(self.tb[self.g], self.ub, GRP)
        self.b3.start()

    def stage4(self):
        self.b3.wait_recv()
        step = self.vb.shape[1]
        for p in range(GRP):
            i, j = p // 2, p % 2
            self.ob[self.d, i * step:(i + 1) * step, j * 128:(j + 1) * 128] = self.vb[p].astype(BF)
        self.b4.start()
        self.a3.wait_recv()
        step = self.va.shape[1]
        for p in range(DOM):
            i, j = p // 2, p % 2
            self.oa[self.g, i * step:(i + 1) * step, j * 128:(j + 1) * 128] = self.va[p].astype(BF)
        self.a4.start()

    def finish(self):
        self.a4.wait_recv()
        self.b4.wait_recv()

    def drain(self):
        for e in (self.a1, self.b1, self.a2, self.b2, self.a3, self.b3, self.a4, self.b4):
            e.wait_send()


def reduce_scratch(rows_a, rows_b):
    ra, rb = rows_a // 8, rows_b // 16
    return [
        pltpu.VMEM((8, ra, W), BF), pltpu.VMEM((8, ra, W), BF),
        pltpu.VMEM((16, ra // 8, 128), F32), pltpu.VMEM((16, ra // 8, 128), F32),
        pltpu.VMEM((16, ra // 8, 128), F32), pltpu.VMEM((8, ra, W), BF),
        pltpu.VMEM((16, rb, W), BF), pltpu.VMEM((16, rb, W), BF),
        pltpu.VMEM((8, rb // 4, 128), F32), pltpu.VMEM((8, rb // 4, 128), F32),
        pltpu.VMEM((8, rb // 4, 128), F32), pltpu.VMEM((16, rb, W), BF),
    ]


def kernel(
    nodes, edges, snd, rcv, cnt, halo, agg, cedges, csnd, crcv, cot, fw, cw,
    fine_out, node_grad, edge_grad, fwg, cwg, *s
):
    (hpad, hr, ohh, outg, hin, m_t, m_n, cps, cpr, wcat, p_r, xcat, act, gpr, yv, rsv, summed,
     an, gn, yn, rsn, refined, rsb, rsr, cinb, ce, cx, cwc, cact, cgp, cy, crs, coutb,
     ssb, ssr, dcinb, rg, dnp, dsm, s_s, s_r, g_ae, g_b, hret, hrin, ssem, rsem, csem,
     arc_s, arc_r, are_s, are_r) = s[:52]
    arc_refs, are_refs = s[52:64], s[64:76]
    d = lax.axis_index("dom")
    g = lax.axis_index("grp")
    count = cnt[0]

    ce_copy = pltpu.make_async_copy(cedges.at[0, pl.ds(pl.multiple_of(g * 512, 512), 512)], ce, csem)
    ce_copy.start()
    barrier = pltpu.get_barrier_semaphore()

    def greet_dom(k, c):
        pl.semaphore_signal(barrier, inc=1, device_id={"dom": lax.rem(d + k, DOM)}, device_id_type=MESH)
        return c

    def greet_grp(k, c):
        pl.semaphore_signal(barrier, inc=1, device_id={"grp": lax.rem(g + k, GRP)}, device_id_type=MESH)
        return c

    lax.fori_loop(1, DOM, greet_dom, 0)
    lax.fori_loop(1, GRP, greet_grp, 0)

    x_halo = Exchange("dom", DOM, d, lambda p: outg.at[p], lambda k: hin.at[d], ssem, rsem, 0)
    x_ret = Exchange("dom", DOM, d, lambda p: hret.at[p], lambda k: hrin.at[d], ssem, rsem, 16)
    x_cp = Exchange("grp", GRP, g, lambda p: cps.at[p], lambda k: cpr.at[k], ssem, rsem, 32)
    x_rs = Exchange("grp", GRP, g, lambda p: rsb.at[p], lambda k: rsr.at[k], ssem, rsem, 40)
    x_cin = Exchange("grp", GRP, g, lambda p: cinb.at[g], lambda k: cinb.at[g], ssem, rsem, 48)
    x_cout = Exchange("grp", GRP, g, lambda p: coutb.at[g], lambda k: coutb.at[g], ssem, rsem, 56)
    x_ss = Exchange("grp", GRP, g, lambda p: ssb.at[p], lambda k: ssr.at[k], ssem, rsem, 64)
    x_dcin = Exchange("grp", GRP, g, lambda p: dcinb.at[g], lambda k: dcinb.at[g], ssem, rsem, 72)
    arc = AllReduce(arc_refs, d, g, arc_s, arc_r)
    are = AllReduce(are_refs, d, g, are_s, are_r)

    lane = iota((128, 128), 1)
    sub = iota((128, 128), 0)

    hpad[...] = jnp.zeros_like(hpad)
    hpad[:, 0:32] = halo[...]
    padded = hpad[...]
    rolled = [padded] + [pltpu.roll(padded, 32 * i, 1) for i in range(1, 4)]
    for j in range(4):
        row = rolled[0][4 * j:4 * j + 1]
        for i in range(1, 4):
            row = row + rolled[i][4 * j + i:4 * j + i + 1]
        hr[j:j + 1, :] = row
        col = column(row)
        for b in range(8):
            ohh[128 * j:128 * j + 128, 128 * b:128 * b + 128] = hot(col == lane + 128 * b)
    outg[...] = mm(ohh[...], nodes[...]).astype(BF).reshape(16, 32, W)
    hin[d] = jnp.zeros((32, W), BF)
    pl.semaphore_wait(barrier, DOM + GRP - 2)
    x_halo.start()

    def member(j, c):
        row = agg[pl.ds(j, 1), :]
        col = column(row)
        at = pl.multiple_of(j * 128, 128)
        for b in range(8):
            m_t[128 * b:128 * b + 128, pl.ds(at, 128)] = hot(sub + 128 * b == row)
            m_n[pl.ds(at, 128), 128 * b:128 * b + 128] = hot(col == lane + 128 * b)
        return c

    lax.fori_loop(0, 8, member, 0)
    cps[...] = mm(m_t[...], cot[...]).astype(BF).reshape(8, 128, W)
    x_cp.start()

    wcat[0:256] = fw[0:256]
    wcat[256:1280] = mm(nodes[...], fw[256:512]).astype(BF)
    p_r[...] = mm(nodes[...], fw[512:768]).astype(BF)
    x_halo.wait_recv()
    wcat[1280:1792] = mm(hin[...].reshape(512, W), fw[256:512]).astype(BF)

    def edge_forward(t, c):
        base = pl.multiple_of(t * 512, 512)
        nbase = pl.multiple_of(t * 128, 128)
        xcat[:, 0:256] = edges[pl.ds(base, 512), :]
        back = []
        for j in range(4):
            srow = snd[pl.ds(4 * t + j, 1), :]
            rrow = rcv[pl.ds(4 * t + j, 1), :] - 128 * t
            scol = column(srow)
            rcol = column(rrow)
            for b in range(12):
                xcat[128 * j:128 * j + 128, 256 + 128 * b:384 + 128 * b] = hot(scol == lane + 128 * b)
            xcat[128 * j:128 * j + 128, 1792:1920] = hot((rcol == lane) & (sub + 128 * j < count))
            back.append(hot((rrow == sub) & (lane + 128 * j < count)))
        wcat[1792:1920] = p_r[pl.ds(nbase, 128), :]
        h = mm(xcat[...], wcat[...])
        a, gp = silu_parts(h)
        act[pl.ds(base, 512), :] = a
        gpr[pl.ds(base, 512), :] = gp
        y, rs = norm(mm(a, fw[768:1024]))
        y = y.astype(BF)
        yv[pl.ds(base, 512), :] = y
        rsv[pl.ds(base, 512), :] = rs
        summed[pl.ds(nbase, 128), :] = mm(jnp.concatenate(back, axis=1), y).astype(BF)
        return c

    lax.fori_loop(0, TILES, edge_forward, 0)

    def node_forward(t, c):
        rows = pl.ds(pl.multiple_of(t * 512, 512), 512)
        h = mm(nodes[rows, :], fw[1024:1280]) + mm(summed[rows, :], fw[1280:1536])
        a, gp = silu_parts(h)
        an[rows, :] = a
        gn[rows, :] = gp
        y, rs = norm(mm(a, fw[1536:1792]))
        yn[rows, :] = y.astype(BF)
        rsn[rows, :] = rs
        refined[rows, :] = (nodes[rows, :].astype(F32) + y).astype(BF)
        return c

    lax.fori_loop(0, 2, node_forward, 0)

    def restrict(k, c):
        p = lax.rem(g + k, GRP)
        part = mm(m_t[pl.ds(pl.multiple_of(p * 128, 128), 128), :], refined[...]) * 0.125
        rsb[p] = part.astype(BF)

        @pl.when(k < GRP)
        def _():
            x_rs.copy(k).start()

        return c

    lax.fori_loop(1, GRP + 1, restrict, 0)
    x_rs.wait_recv()
    cin = summed_blocks(rsb[g], rsr, GRP).astype(BF)
    cinb[g] = cin
    x_cin.start()

    ce_copy.wait()
    cx[:, 0:256] = ce[...]
    cback = []
    for j in range(4):
        srow = csnd[pl.ds(4 * g + j, 1), :]
        rrow = crcv[pl.ds(4 * g + j, 1), :]
        scol = column(srow)
        rcol = column(rrow)
        for b in range(8):
            cx[128 * j:128 * j + 128, 256 + 128 * b:384 + 128 * b] = hot(scol == lane + 128 * b)
        cx[128 * j:128 * j + 128, 1280:1408] = hot(rcol == lane)
        cback.append(hot(rrow == sub))
    cback = jnp.concatenate(cback, axis=1)
    cwc[0:256] = cw[0:256]
    cwc[1280:1408] = mm(cin, cw[512:768]).astype(BF)
    x_cp.wait_recv()
    pg = summed_blocks(cps[g], cpr, GRP).astype(BF).astype(F32)
    x_cin.wait_recv()
    cwc[256:1280] = mm(cinb[...].reshape(1024, W), cw[256:512]).astype(BF)
    ca, cg = silu_parts(mm(cx[...], cwc[...]))
    cact[...] = ca
    cgp[...] = cg
    y, rs = norm(mm(ca, cw[768:1024]))
    y = y.astype(BF)
    cy[...] = y
    crs[...] = rs
    csum = mm(cback, y).astype(BF)
    cna, cng = silu_parts(mm(cin, cw[1024:1280]) + mm(csum, cw[1280:1536]))
    cny, cnrs = norm(mm(cna, cw[1536:1792]))
    coutb[g] = (cin.astype(F32) + cny).astype(BF)
    x_cout.start()

    cndz = norm_back(pg, cny, cnrs)
    cndh = (mm_nt(cndz, cw[1536:1792]) * cng.astype(F32)).astype(BF)
    dcin_part = pg + mm_nt(cndh, cw[1024:1280])
    dcsum = mm_nt(cndh, cw[1280:1536]).astype(BF)
    cdz = norm_back(mm(cx[:, 1280:1408], dcsum), cy[...].astype(F32), crs[...])
    cdh = (mm_nt(cdz, cw[768:1024]) * cgp[...].astype(F32)).astype(BF)
    gp = cgp
    gp[...] = cdh

    def sender_sum(k, c):
        p = lax.rem(g + k, GRP)
        rows = [hot(csnd[pl.ds(4 * g + j, 1), :] - 128 * p == sub) for j in range(4)]
        ssb[p] = mm(jnp.concatenate(rows, axis=1), gp[...]).astype(BF)

        @pl.when(k < GRP)
        def _():
            x_ss.copy(k).start()

        return c

    lax.fori_loop(1, GRP + 1, sender_sum, 0)
    s_cr = mm(cback, cdh).astype(BF)

    def put_a(at, value):
        value = value.astype(BF)
        for b in range(2):
            arc.sa[at // 128 + b] = value[128 * b:128 * b + 128]

    def put_b(at, value):
        value = value.astype(BF)
        pos = 0
        while pos < 256:
            block, inside = (at + pos) // 96, (at + pos) % 96
            n = min(96 - inside, 256 - pos)
            arc.sb[block, inside:inside + n, :] = value[pos:pos + n]
            pos += n

    put_a(0, mm_tn(ce[...], cdh))
    put_a(768, mm_tn(cact[...], cdz))
    put_b(0, mm_tn(cin, cndh))
    put_b(256, mm_tn(csum, cndh))
    put_b(512, mm_tn(cna, cndz))
    dcin_part = dcin_part + mm_nt(s_cr, cw[512:768])
    x_ss.wait_recv()
    s_tot = summed_blocks(ssb[g], ssr, GRP).astype(BF)
    dcinb[g] = (dcin_part + mm_nt(s_tot, cw[256:512])).astype(BF)
    x_dcin.start()
    put_a(256, mm_tn(cin, s_tot))
    put_a(512, mm_tn(cin, s_cr))

    x_cout.wait_recv()
    fine_out[...] = (refined[...].astype(F32) + mm(m_n[...], coutb[...].reshape(1024, W))).astype(BF)
    x_dcin.wait_recv()
    rg[...] = (cot[...].astype(F32) + 0.125 * mm(m_n[...], dcinb[...].reshape(1024, W))).astype(BF)

    dz = norm_back(rg[...].astype(F32), yn[...].astype(F32), rsn[...])
    dh = (mm_nt(dz, fw[1536:1792]) * gn[...].astype(F32)).astype(BF)
    dnp[...] = rg[...].astype(F32) + mm_nt(dh, fw[1024:1280])
    dsm[...] = mm_nt(dh, fw[1280:1536]).astype(BF)
    put_b(768, mm_tn(nodes[...], dh))
    put_b(1024, mm_tn(summed[...], dh))
    put_b(1280, mm_tn(an[...], dz))
    arc.stage1()

    s_s[...] = jnp.zeros_like(s_s)
    g_ae[...] = jnp.zeros_like(g_ae)
    g_b[...] = jnp.zeros_like(g_b)

    def edge_backward(t, c):
        base = pl.multiple_of(t * 512, 512)
        nbase = pl.multiple_of(t * 128, 128)
        cols, back, srows = [], [], []
        for j in range(4):
            rrow = rcv[pl.ds(4 * t + j, 1), :] - 128 * t
            cols.append(hot((column(rrow) == lane) & (sub + 128 * j < count)))
            back.append(hot((rrow == sub) & (lane + 128 * j < count)))
            srows.append(snd[pl.ds(4 * t + j, 1), :])
        dmsg = mm(jnp.concatenate(cols, axis=0), dsm[pl.ds(nbase, 128), :])
        dz = norm_back(dmsg, yv[pl.ds(base, 512), :].astype(F32), rsv[pl.ds(base, 512), :])
        dh = (mm_nt(dz, fw[768:1024]) * gpr[pl.ds(base, 512), :].astype(F32)).astype(BF)
        edge_grad[pl.ds(base, 512), :] = mm_nt(dh, fw[0:256]).astype(BF)
        g_b[...] += mm_tn(act[pl.ds(base, 512), :], dz)
        g_ae[...] += mm_tn(edges[pl.ds(base, 512), :], dh)
        s_r[pl.ds(nbase, 128), :] = mm(jnp.concatenate(back, axis=1), dh).astype(BF)
        for b in range(12):
            block = jnp.concatenate([hot(srow - 128 * b == sub) for srow in srows], axis=1)
            s_s[128 * b:128 * b + 128, :] += mm(block, dh)
        return c

    lax.fori_loop(0, TILES // 2, edge_backward, 0)
    arc.stage2()
    lax.fori_loop(TILES // 2, TILES, edge_backward, 0)

    ss = s_s[...].astype(BF)
    hret[...] = mm_nt(ss[1024:1536], fw[256:512]).astype(BF).reshape(16, 32, W)
    x_ret.start()
    for b in range(4):
        are.sa[b] = g_ae[64 * b:64 * b + 64].astype(BF)
    g_as = (mm_tn(nodes[...], ss[0:1024]) + mm_tn(hin[...].reshape(512, W), ss[1024:1536])).astype(BF)
    for b in range(4):
        are.sa[4 + b] = g_as[64 * b:64 * b + 64]
    g_ar = mm_tn(nodes[...], s_r[...]).astype(BF)
    for b in range(8):
        are.sb[b] = g_ar[32 * b:32 * b + 32]
        are.sb[8 + b] = g_b[32 * b:32 * b + 32].astype(BF)
    are.stage1()
    arc.stage3()
    own = dnp[...] + mm_nt(ss[0:1024], fw[256:512]) + mm_nt(s_r[...], fw[512:768])
    hrin[d] = jnp.zeros((32, W), BF)
    x_ret.wait_recv()
    node_grad[...] = (own + mm_tn(ohh[...], hrin[...].reshape(512, W))).astype(BF)
    are.stage2()
    arc.stage4()
    are.stage3()
    are.stage4()
    arc.finish()
    cwg[0:1024] = arc.oa[...].reshape(1024, W).astype(F32) * COARSE_SCALE
    cwg[1024:1792] = arc.ob[0:8].reshape(768, W).astype(F32) * COARSE_SCALE
    fwg[1024:1792] = arc.ob[8:16].reshape(768, W).astype(F32) * FINE_SCALE
    are.finish()
    fwg[0:512] = are.oa[...].reshape(512, W).astype(F32) * FINE_SCALE
    fwg[512:1024] = are.ob[...].reshape(512, W).astype(F32) * FINE_SCALE

    for x in (x_halo, x_ret, x_cp, x_rs, x_cin, x_cout, x_ss, x_dcin):
        x.wait_send()
    arc.drain()
    are.drain()


def body(
    nodes, edges, senders, receivers, edge_count, halo_rows, aggregates,
    coarse_edges, coarse_senders, coarse_receivers, cotangent, fine_weights, coarse_weights,
):
    vm = pl.BlockSpec(memory_space=pltpu.VMEM)
    V = pltpu.VMEM
    scratch = [
        V((16, 128), jnp.int32),
        V((8, 128), jnp.int32),
        V((512, 1024), BF),
        V((16, 32, W), BF),
        V((16, 32, W), BF),
        V((1024, 1024), BF),
        V((1024, 1024), BF),
        V((8, 128, W), BF),
        V((8, 128, W), BF),
        V((1920, W), BF),
        V((1024, W), BF),
        V((512, 1920), BF),
        V((4096, W), BF),
        V((4096, W), BF),
        V((4096, W), BF),
        V((4096, 1), F32),
        V((1024, W), BF),
        V((1024, W), BF),
        V((1024, W), BF),
        V((1024, W), BF),
        V((1024, 1), F32),
        V((1024, W), BF),
        V((8, 128, W), BF),
        V((8, 128, W), BF),
        V((8, 128, W), BF),
        V((512, W), BF),
        V((512, 1408), BF),
        V((1408, W), BF),
        V((512, W), BF),
        V((512, W), BF),
        V((512, W), BF),
        V((512, 1), F32),
        V((8, 128, W), BF),
        V((8, 128, W), BF),
        V((8, 128, W), BF),
        V((8, 128, W), BF),
        V((1024, W), BF),
        V((1024, W), F32),
        V((1024, W), BF),
        V((1536, W), F32),
        V((1024, W), BF),
        V((256, W), F32),
        V((256, W), F32),
        V((16, 32, W), BF),
        V((16, 32, W), BF),
        pltpu.SemaphoreType.DMA((80,)),
        pltpu.SemaphoreType.DMA((80,)),
        pltpu.SemaphoreType.DMA,
        pltpu.SemaphoreType.DMA((96,)),
        pltpu.SemaphoreType.DMA((96,)),
        pltpu.SemaphoreType.DMA((96,)),
        pltpu.SemaphoreType.DMA((96,)),
    ] + reduce_scratch(1024, 1536) + reduce_scratch(512, 512)
    return pl.pallas_call(
        kernel,
        out_shape=(
            jax.ShapeDtypeStruct((1024, W), BF),
            jax.ShapeDtypeStruct((1024, W), BF),
            jax.ShapeDtypeStruct((4096, W), BF),
            jax.ShapeDtypeStruct((1792, W), F32),
            jax.ShapeDtypeStruct((1792, W), F32),
        ),
        in_specs=[vm, vm, vm, vm, pl.BlockSpec(memory_space=pltpu.SMEM), vm, vm,
                  pl.BlockSpec(memory_space=pl.ANY), vm, vm, vm, vm, vm],
        out_specs=(vm,) * 5,
        scratch_shapes=scratch,
        compiler_params=pltpu.CompilerParams(
            collective_id=0, has_side_effects=True, vmem_limit_bytes=60 * 1024 * 1024
        ),
    )(
        nodes, edges, senders.reshape(32, 128), receivers.reshape(32, 128), edge_count,
        halo_rows.reshape(16, 32), aggregates.reshape(8, 128), coarse_edges,
        coarse_senders.reshape(32, 128), coarse_receivers.reshape(32, 128), cotangent,
        fine_weights, coarse_weights,
    )


def solution(mesh):
    both = ("dom", "grp")
    placed = (
        P(both, None), P(both, None), P(both), P(both), P(both), P(both, None, None), P(both),
        P("dom", None, None), P("dom", None), P("dom", None), P(both, None), P(), P(),
    )
    return jax.shard_map(
        body, mesh=mesh, in_specs=placed,
        out_specs=(P(both, None), P(both, None), P(both, None), P(), P()),
        check_vma=False,
    )
```

time: 574 us -> 138 us (0.24); the launches traced: 563 us -> 138 us
  waiting for transfers between devices: 212 us -> 0 us
  other arithmetic: 139 us -> 0 us
  Pallas kernels: 0 us -> 127 us
  local copies, waits for them, and re-layouts: 109 us -> 9.53 us
  matrix products: 71.3 us -> 0 us
  starting transfers between devices: 15.2 us -> 0 us
  between operations: 15.9 us -> 1.3 us
    psum x3 -> x0, waiting for transfers between devices: 208 us -> none  [the longest x1 83.3 us: body(): lax.psum(coarse_grad.astype(jnp.bfloat16), 'dom').astype(jnp.float32)]
    pallas_call x0 -> x1, Pallas kernels: none -> 127 us  [body(): pl.pallas_call(kernel, out_shape=(jax.ShapeDtypeStruct((1024, W), BF), ja...]
    scatter-add x5 -> x0, other arithmetic: 97.4 us -> none  [the longest x1 25.2 us: fine_part(): target_rows = jnp.take(node_wide, receivers, axis=0).astype(jnp.bfloat16)]
    dot_general x32 -> x0, matrix products: 71.3 us -> none  [the longest x12 26.8 us: two_layer(): hidden = jnp.dot(inputs, first, preferred_element_type=jnp.float32)]
    gather x5 -> x0, local copies, waits for them, and re-layouts: 70.9 us -> none  [the longest x1 17.3 us: coarse_layer(): jnp.take(source_rows, local_index, axis=0).astype(jnp.bfloat16)]
    all_to_all x2 -> x0, starting transfers between devices: 15.1 us -> none  [the longest x1 8.43 us: body(): lax.all_to_all(outgoing, 'dom', split_axis=0, concat_axis=0, tiled=True)]
    convert_element_type x9 -> x0, other arithmetic: 13.9 us -> none  [the longest x1 5.31 us: fine_part(): target_rows = jnp.take(node_wide, receivers, axis=0).astype(jnp.bfloat16)]
    reshape x8 -> x0, local copies, waits for them, and re-layouts: 13.6 us -> none  [the longest x2 6.99 us: tile_sum(): messages.reshape(tile_count, per_tile, -1)]
  transfers between devices with their start and end apart: 5 -> 0, of which waited for: 4 -> 0; matrix products, arithmetic and copies ran while one was open for 16% -> 0% of each run, Pallas kernels for 0% -> 0%
where the time goes in v1:
time: 138 us
  Pallas kernels  127 us (92%)
  local copies, waits for them, and re-layouts  9.53 us (7%)
    pallas_call x1, Pallas kernels, body(): pl.pallas_call(kernel, out_shape=(jax.ShapeDtypeStruct((1024, W), BF), ja...  127 us
    unnamed x11, local copies, waits for them, and re-layouts  9.53 us

profile of v1, /device:TPU:1, one launch (start us, length us, event | category | flops | bytes accessed | tf_op | source)
XLA Modules:
  0.0 137.8 jit_solution(10769499253720917796)
XLA Ops:
  1.3 126.9 %shard_map.164 = (bf16[1024,256]{1,0:T(8,128)(2,1)}, bf16[1024,256]{1,0:T(8,128)(2,1)}, bf16[4096,256]{1,0:T(8,128)(2,1)}, f32[1792,256]{1,0:T(8,128)}, f32[1792,256]{1,0:T(8,128)}) custom-call(bf16[1024,256]{1,0:T(8,128)(2,1)} %nodes.1, bf16[4096,256]{1,0:T(8,128)(2,1)} %edges.1, s32[32,128]{1,0:T(8,128)} %bitcast.6, s32[32,128]{1,0:T(8,128)} %bitcast.7, ...), custom_call_target="tpu_custom_call" | custom-call | tf_op jit(solution)/shard_map/pallas_call | solution.py:540
  128.2 0.0 copy-start
  128.2 2.0 %copy.24 = bf16[1024,256]{1,0:T(8,128)(2,1)} copy(bf16[1024,256]{1,0:T(8,128)(2,1)} %get-tuple-element.10) | data formatting | bytes 1048576
  130.2 1.9 %copy.25 = bf16[1024,256]{1,0:T(8,128)(2,1)} copy(bf16[1024,256]{1,0:T(8,128)(2,1)} %get-tuple-element.11) | data formatting | bytes 1048576
  132.1 0.0 copy-done
  132.1 0.0 copy-start.2
  132.1 1.3 copy.26
  133.4 0.9 copy-done.2
  134.4 0.0 copy-start.1
  134.4 1.2 copy.27
  135.6 0.9 copy-done.1
  136.5 1.2 copy.28
Async XLA Ops:
  128.2 3.9 %copy-start = (bf16[4096,256]{1,0:T(8,128)(2,1)S(1)}, bf16[4096,256]{1,0:T(8,128)(2,1)}, u32[]{:S(2)}) copy-start(bf16[4096,256]{1,0:T(8,128)(2,1)} %get-tuple-element.12) | copy-start | bytes 6291460
  132.1 2.3 %copy-start.2 = (f32[1792,256]{1,0:T(8,128)S(1)}, f32[1792,256]{1,0:T(8,128)}, u32[]{:S(2)}) copy-start(f32[1792,256]{1,0:T(8,128)} %get-tuple-element.13) | copy-start | bytes 5505028
  134.4 2.2 %copy-start.1 = (f32[1792,256]{1,0:T(8,128)S(1)}, f32[1792,256]{1,0:T(8,128)}, u32[]{:S(2)}) copy-start(f32[1792,256]{1,0:T(8,128)} %get-tuple-element.14) | copy-start | bytes 5505028

commit v2 on v1

v2 whole, which is shorter than its diff:
```python
import jax
import jax.numpy as jnp
from jax import lax
from jax.experimental import pallas as pl
from jax.experimental.pallas import tpu as pltpu
from jax.sharding import PartitionSpec as P

MESH = pl.DeviceIdType.MESH
BF = jnp.bfloat16
F32 = jnp.float32
W = 256
DOM = 16
GRP = 8
TILES = 8
YS = 4
FINE_SCALE = 524288 ** (-0.5)
COARSE_SCALE = 65536 ** (-0.5)


def mm(a, b):
    return jnp.dot(a, b, preferred_element_type=F32)


def mm_nt(a, b):
    return lax.dot_general(a, b, (((1,), (1,)), ((), ())), preferred_element_type=F32)


def mm_tn(a, b):
    return lax.dot_general(a, b, (((0,), (0,)), ((), ())), preferred_element_type=F32)


def iota(shape, axis):
    return lax.broadcasted_iota(jnp.int32, shape, axis)


def hot(mask):
    return jnp.where(mask, 1.0, 0.0).astype(BF)


def column(row):
    return jnp.broadcast_to(row, (128, 128)).T


def silu_parts(h):
    sig = 1.0 / (1.0 + jnp.exp(-h))
    active = h * sig
    return active.astype(BF), (sig * (1.0 + h - active)).astype(BF)


def norm(z):
    centre = z - jnp.mean(z, axis=-1, keepdims=True)
    rs = lax.rsqrt(jnp.mean(centre * centre, axis=-1, keepdims=True) + 1e-05)
    return centre * rs, rs


def norm_back(dy, y, rs):
    first = jnp.mean(dy, axis=-1, keepdims=True)
    second = jnp.mean(dy * y, axis=-1, keepdims=True)
    return (rs * (dy - first - y * second)).astype(BF)


class Links:
    def __init__(self, ssem, rsem):
        self.d, self.g = lax.axis_index("dom"), lax.axis_index("grp")
        self.y, self.core = self.g // 2, lax.rem(self.g, 2)
        self.ssem, self.rsem, self.used = ssem, rsem, 0
        self.all = []

    def exchange(self, kind, src, dst):
        x = Exchange(self, kind, src, dst, self.used)
        self.used += x.count
        self.all.append(x)
        return x


class Exchange:
    def __init__(self, at, kind, src, dst, off):
        self.at, self.kind, self.src, self.dst, self.off = at, kind, src, dst, off
        self.count = {"dom": DOM, "grp": GRP, "y": YS, "mate": 2}[kind]

    def copy(self, k):
        at = self.at
        if self.kind == "dom":
            p = lax.rem(at.d + k, DOM)
            device = {"dom": p}
        elif self.kind == "grp":
            p = lax.rem(at.g + k, GRP)
            device = {"grp": p}
        elif self.kind == "y":
            p = lax.rem(at.y + k, YS)
            device = {"grp": 2 * p + at.core}
        else:
            p = 1 - at.core
            device = {"grp": 2 * at.y + p}
        return pltpu.make_async_remote_copy(
            src_ref=self.src(p),
            dst_ref=self.dst(k),
            send_sem=self.at.ssem.at[self.off + k],
            recv_sem=self.at.rsem.at[self.off + k],
            device_id=device,
            device_id_type=MESH,
        )

    def each(self, act):
        def step(k, carry):
            act(self.copy(k))
            return carry

        if self.count <= YS:
            for k in range(1, self.count):
                step(k, 0)
        else:
            lax.fori_loop(1, self.count, step, 0)

    def start(self):
        self.each(lambda c: c.start())

    def wait_recv(self):
        self.each(lambda c: c.wait_recv())

    def wait_send(self):
        self.each(lambda c: c.wait_send())


def total_of(first, blocks, which):
    total = first.astype(F32)
    for k in which:
        total = total + blocks[k].astype(F32)
    return total


class GroupSum:
    def __init__(self, links, s, m, t, r):
        self.links, self.s, self.m, self.t, self.r = links, s, m, t, r
        self.first = links.exchange("mate", lambda p: s.at[p], lambda k: m)
        self.second = links.exchange("y", lambda p: t.at[p], lambda k: r.at[k])

    def pair(self):
        self.first.wait_recv()
        self.t[...] = (self.s[self.links.core].astype(F32) + self.m[...].astype(F32)).astype(BF)
        self.second.start()

    def result(self):
        self.second.wait_recv()
        return total_of(self.t[self.links.y], self.r, range(1, YS))


class GroupGather:
    def __init__(self, links, b):
        self.links, self.b = links, b
        g, y, core = links.g, links.y, links.core
        self.mate = links.exchange("mate", lambda p: b.at[g], lambda k: b.at[g])
        self.far = links.exchange("y", lambda p: b.at[g], lambda k: b.at[g])
        self.passed = []
        for k in range(1, YS):
            p = 2 * lax.rem(y + YS - k, YS) + core
            self.passed.append(links.exchange("mate", lambda q, p=p: b.at[p], lambda q, p=p: b.at[p]))

    def start(self):
        self.far.start()
        self.mate.start()

    def wait_recv(self):
        for k in range(1, YS):
            self.far.copy(k).wait_recv()
            self.passed[k - 1].start()
        self.mate.wait_recv()
        for x in self.passed:
            x.wait_recv()


class EarlySum:
    def __init__(self, links, s, m, t, r, v, o):
        self.links, self.s, self.m, self.t, self.r, self.v, self.o = links, s, m, t, r, v, o
        d, y, core = links.d, links.y, links.core
        self.x0 = links.exchange("mate", lambda p: s.at[p], lambda k: m)
        self.x1 = links.exchange("dom", lambda p: t.at[p], lambda k: r.at[k])
        self.x2 = links.exchange("y", lambda p: v.at[y], lambda k: v.at[y])
        self.x3 = links.exchange("dom", lambda p: o.at[core, d], lambda k: o.at[core, d])
        self.x4 = links.exchange("mate", lambda p: o.at[core], lambda k: o.at[core])

    def stage0(self):
        self.x0.start()

    def stage1(self):
        self.x0.wait_recv()
        self.t[...] = (self.s[self.links.core].astype(F32) + self.m[...].astype(F32)).astype(BF)
        self.x1.start()

    def stage2(self):
        self.x1.wait_recv()
        self.v[self.links.y] = total_of(self.t[self.links.d], self.r, range(1, DOM)).astype(BF)
        self.x2.start()

    def stage3(self):
        self.x2.wait_recv()
        self.o[self.links.core, self.links.d] = total_of(self.v[0], self.v, range(1, YS)).astype(BF)
        self.x3.start()

    def stage4(self):
        self.x3.wait_recv()
        self.x4.start()

    def finish(self):
        self.x4.wait_recv()


class LateSum:
    def __init__(self, links, sa, ra, va, oa, sb, rb, vb, ob):
        self.links = links
        self.sa, self.ra, self.va, self.oa = sa, ra, va, oa
        self.sb, self.rb, self.vb, self.ob = sb, rb, vb, ob
        d, g = links.d, links.g
        self.a1 = links.exchange("grp", lambda p: sa.at[p], lambda k: ra.at[k])
        self.b1 = links.exchange("dom", lambda p: sb.at[p], lambda k: rb.at[k])
        self.a2 = links.exchange("dom", lambda p: va.at[d], lambda k: va.at[d])
        self.b2 = links.exchange("grp", lambda p: vb.at[g], lambda k: vb.at[g])
        self.a3 = links.exchange("grp", lambda p: oa.at[g], lambda k: oa.at[g])
        self.b3 = links.exchange("dom", lambda p: ob.at[d], lambda k: ob.at[d])

    def stage2(self):
        d, g = self.links.d, self.links.g
        self.a1.wait_recv()
        self.va[d] = total_of(self.sa[g], self.ra, range(1, GRP)).astype(BF)
        self.a2.start()
        self.b1.wait_recv()
        self.vb[g] = total_of(self.sb[d], self.rb, range(1, DOM)).astype(BF)
        self.b2.start()

    def stage3(self):
        d, g = self.links.d, self.links.g
        self.b2.wait_recv()
        self.ob[d] = total_of(self.vb[0], self.vb, range(1, GRP)).astype(BF)
        self.b3.start()
        self.a2.wait_recv()
        self.oa[g] = total_of(self.va[0], self.va, range(1, DOM)).astype(BF)
        self.a3.start()

    def finish(self):
        self.a3.wait_recv()
        self.b3.wait_recv()


def put(ref, lead, at, value):
    value = value.astype(BF)
    rows, pos = ref.shape[-2], 0
    while pos < value.shape[0]:
        block, inside = (at + pos) // rows, (at + pos) % rows
        n = min(rows - inside, value.shape[0] - pos)
        ref[lead(block) + (slice(inside, inside + n), slice(None))] = value[pos:pos + n]
        pos += n


def halves(block):
    return (block // DOM, block % DOM)


def single(block):
    return (block,)


def kernel(
    nodes_h, edges_h, snd, rcv, cnt, halo, agg, cedges_h, csnd, crcv, cot_h, fw_h, cw_h,
    fine_out_h, node_grad_h, edge_grad_h, grads_h, *s
):
    (nodes, edges, cot, fw, cw, ce, fine_out, node_grad,
     hpad, hr, ohh, outg, hin, m_t, m_n, oh, wcat, p_r, act, gpr, yv, rsv, summed,
     an, gn, yn, rsn, refined, cinb, cx, cwc, cact, cgp, cy, crs, coutb,
     dcinb, rg, dnp, dsm, s_s, s_r, g_ae, g_b, hret, hrin, ssem, rsem, isem, osem) = s[:50]
    rest = list(s[50:])
    edge_grad, staged = yv, act

    def take(n):
        out = rest[:n]
        del rest[:n]
        return out

    links = Links(ssem, rsem)
    d, g, y, core = links.d, links.g, links.y, links.core
    count = cnt[0]

    loads = [
        pltpu.make_async_copy(src, dst, isem.at[i])
        for i, (src, dst) in enumerate((
            (nodes_h, nodes), (fw_h, fw), (cot_h, cot), (edges_h, edges), (cw_h, cw),
            (cedges_h.at[0, pl.ds(pl.multiple_of(g * 512, 512), 512)], ce),
        ))
    ]
    for c in loads:
        c.start()
    ld_nodes, ld_fw, ld_cot, ld_edges, ld_cw, ld_ce = loads
    barrier = pltpu.get_barrier_semaphore()

    def greet_dom(k, c):
        pl.semaphore_signal(barrier, inc=1, device_id={"dom": lax.rem(d + k, DOM)}, device_id_type=MESH)
        return c

    def greet_grp(k, c):
        pl.semaphore_signal(barrier, inc=1, device_id={"grp": lax.rem(g + k, GRP)}, device_id_type=MESH)
        return c

    lax.fori_loop(1, DOM, greet_dom, 0)
    lax.fori_loop(1, GRP, greet_grp, 0)

    x_halo = links.exchange("dom", lambda p: outg.at[p], lambda k: hin.at[d])
    x_ret = links.exchange("dom", lambda p: hret.at[p], lambda k: hrin.at[d])
    pro = GroupSum(links, *take(4))
    res = GroupSum(links, *take(4))
    sen = GroupSum(links, *take(4))
    x_cin = GroupGather(links, cinb)
    x_cout = GroupGather(links, coutb)
    x_dcin = GroupGather(links, dcinb)
    early = EarlySum(links, *take(6))
    middle = EarlySum(links, *take(6))
    late = LateSum(links, *take(8))

    lane = iota((128, 128), 1)
    sub = iota((128, 128), 0)

    hpad[...] = jnp.zeros_like(hpad)
    hpad[:, 0:32] = halo[...]
    padded = hpad[...]
    rolled = [padded] + [pltpu.roll(padded, 32 * i, 1) for i in range(1, 4)]
    for j in range(4):
        row = rolled[0][4 * j:4 * j + 1]
        for i in range(1, 4):
            row = row + rolled[i][4 * j + i:4 * j + i + 1]
        hr[j:j + 1, :] = row
        col = column(row)
        for b in range(8):
            ohh[128 * j:128 * j + 128, 128 * b:128 * b + 128] = hot(col == lane + 128 * b)
    hin[d] = jnp.zeros((32, W), BF)
    hrin[d] = jnp.zeros((32, W), BF)
    ld_nodes.wait()
    outg[...] = mm(ohh[...], nodes[...]).astype(BF).reshape(16, 32, W)
    pl.semaphore_wait(barrier, DOM + GRP - 2)
    x_halo.start()

    def member(j, c):
        row = agg[pl.ds(j, 1), :]
        col = column(row)
        at = pl.multiple_of(j * 128, 128)
        for b in range(8):
            m_t[b % 2, 128 * (b // 2):128 * (b // 2) + 128, pl.ds(at, 128)] = hot(sub + 128 * b == row)
            m_n[pl.ds(at, 128), 128 * b:128 * b + 128] = hot(col == lane + 128 * b)
        return c

    lax.fori_loop(0, 8, member, 0)
    ld_cot.wait()
    for h in range(2):
        pro.s[h] = mm(m_t[h], cot[...]).astype(BF).reshape(YS, 128, W)
    pro.first.start()

    ld_fw.wait()
    wcat[0:256] = fw[0:256]
    wcat[256:1280] = mm(nodes[...], fw[256:512]).astype(BF)
    p_r[...] = mm(nodes[...], fw[512:768]).astype(BF)

    def edge_hot(t, c):
        for j in range(4):
            rows = slice(128 * j, 128 * j + 128)
            scol = column(snd[pl.ds(4 * t + j, 1), :])
            rcol = column(rcv[pl.ds(4 * t + j, 1), :] - 128 * t)
            for b in range(12):
                oh[t, b, rows, :] = hot(scol == lane + 128 * b)
            oh[t, 12, rows, :] = hot((rcol == lane) & (sub + 128 * j < count))
        return c

    lax.fori_loop(0, TILES, edge_hot, 0)
    pro.pair()
    ld_edges.wait()
    x_halo.wait_recv()
    wcat[1280:1792] = mm(hin[...].reshape(512, W), fw[256:512]).astype(BF)

    def edge_forward(t, c):
        base = pl.multiple_of(t * 512, 512)
        nbase = pl.multiple_of(t * 128, 128)
        back = []
        for j in range(4):
            rrow = rcv[pl.ds(4 * t + j, 1), :] - 128 * t
            back.append(hot((rrow == sub) & (lane + 128 * j < count)))
        wcat[1792:1920] = p_r[pl.ds(nbase, 128), :]
        joined = jnp.concatenate([edges[pl.ds(base, 512), :]] + [oh[t, b] for b in range(13)], axis=1)
        h = mm(joined, wcat[...])
        a, gp = silu_parts(h)
        act[pl.ds(base, 512), :] = a
        gpr[pl.ds(base, 512), :] = gp
        y, rs = norm(mm(a, fw[768:1024]))
        y = y.astype(BF)
        yv[pl.ds(base, 512), :] = y
        rsv[pl.ds(base, 512), :] = rs
        summed[pl.ds(nbase, 128), :] = mm(jnp.concatenate(back, axis=1), y).astype(BF)
        return c

    lax.fori_loop(0, TILES, edge_forward, 0)

    def node_forward(t, c):
        rows = pl.ds(pl.multiple_of(t * 512, 512), 512)
        h = mm(nodes[rows, :], fw[1024:1280]) + mm(summed[rows, :], fw[1280:1536])
        a, gp = silu_parts(h)
        an[rows, :] = a
        gn[rows, :] = gp
        y, rs = norm(mm(a, fw[1536:1792]))
        yn[rows, :] = y.astype(BF)
        rsn[rows, :] = rs
        refined[rows, :] = (nodes[rows, :].astype(F32) + y).astype(BF)
        return c

    lax.fori_loop(0, 2, node_forward, 0)

    res.s[1 - core] = (mm(m_t[1 - core], refined[...]) * 0.125).astype(BF).reshape(YS, 128, W)
    res.first.start()
    res.s[core] = (mm(m_t[core], refined[...]) * 0.125).astype(BF).reshape(YS, 128, W)
    res.pair()

    def edge_hot_back(t, c):
        for j in range(4):
            rows = slice(128 * j, 128 * j + 128)
            srow = snd[pl.ds(4 * t + j, 1), :]
            rrow = rcv[pl.ds(4 * t + j, 1), :] - 128 * t
            for b in range(12):
                oh[t, b, rows, :] = hot(srow == sub + 128 * b)
            oh[t, 12, rows, :] = hot((rrow == sub) & (lane + 128 * j < count))
        return c

    ld_ce.wait()
    ld_cw.wait()
    cx[:, 0:256] = ce[...]
    cback = []
    for j in range(4):
        srow = csnd[pl.ds(4 * g + j, 1), :]
        rrow = crcv[pl.ds(4 * g + j, 1), :]
        scol = column(srow)
        rcol = column(rrow)
        for b in range(8):
            cx[128 * j:128 * j + 128, 256 + 128 * b:384 + 128 * b] = hot(scol == lane + 128 * b)
        cx[128 * j:128 * j + 128, 1280:1408] = hot(rcol == lane)
        cback.append(hot(rrow == sub))
    cback = jnp.concatenate(cback, axis=1)
    cwc[0:256] = cw[0:256]
    pg = pro.result().astype(BF).astype(F32)
    lax.fori_loop(0, 3, edge_hot_back, 0)
    cin = res.result().astype(BF)
    cinb[g] = cin
    x_cin.start()
    cwc[1280:1408] = mm(cin, cw[512:768]).astype(BF)
    lax.fori_loop(3, TILES, edge_hot_back, 0)
    x_cin.wait_recv()
    cwc[256:1280] = mm(cinb[...].reshape(1024, W), cw[256:512]).astype(BF)
    ca, cg = silu_parts(mm(cx[...], cwc[...]))
    cact[...] = ca
    cgp[...] = cg
    cyn, rs = norm(mm(ca, cw[768:1024]))
    cyn = cyn.astype(BF)
    cy[...] = cyn
    crs[...] = rs
    csum = mm(cback, cyn).astype(BF)
    cna, cng = silu_parts(mm(cin, cw[1024:1280]) + mm(csum, cw[1280:1536]))
    cny, cnrs = norm(mm(cna, cw[1536:1792]))
    coutb[g] = (cin.astype(F32) + cny).astype(BF)

    cndz = norm_back(pg, cny, cnrs)
    cndh = (mm_nt(cndz, cw[1536:1792]) * cng.astype(F32)).astype(BF)
    dcin_part = pg + mm_nt(cndh, cw[1024:1280])
    dcsum = mm_nt(cndh, cw[1280:1536]).astype(BF)
    cdz = norm_back(mm(cx[:, 1280:1408], dcsum), cy[...].astype(F32), crs[...])
    cdh = (mm_nt(cdz, cw[768:1024]) * cgp[...].astype(F32)).astype(BF)

    def sender_sum(half):
        blocks = []
        for p in range(YS):
            at = 128 * (2 * p + half)
            blocks.append(jnp.concatenate(
                [hot(csnd[pl.ds(4 * g + j, 1), :] - at == sub) for j in range(4)], axis=1))
        sen.s[half] = mm(jnp.concatenate(blocks, axis=0), cdh).astype(BF).reshape(YS, 128, W)

    sender_sum(1 - core)
    sen.first.start()
    sender_sum(core)
    s_cr = mm(cback, cdh).astype(BF)
    sen.pair()
    x_cout.start()
    put(early.s, halves, 0, mm_tn(ce[...], cdh))
    put(early.s, halves, 256, mm_tn(cact[...], cdz))
    put(early.s, halves, 512, mm_tn(cin, cndh))
    put(early.s, halves, 768, mm_tn(csum, cndh))
    put(early.s, halves, 1024, mm_tn(cna, cndz))
    put(middle.s, halves, 0, mm_tn(cin, s_cr))
    dcin_part = dcin_part + mm_nt(s_cr, cw[512:768])
    s_tot = sen.result().astype(BF)
    dcinb[g] = (dcin_part + mm_nt(s_tot, cw[256:512])).astype(BF)
    x_dcin.start()
    put(early.s, halves, 1280, mm_tn(cin, s_tot))
    early.stage0()

    x_cout.wait_recv()
    fine_out[...] = (refined[...].astype(F32) + mm(m_n[...], coutb[...].reshape(1024, W))).astype(BF)
    st_fine = pltpu.make_async_copy(fine_out, fine_out_h, osem.at[0])
    st_fine.start()
    early.stage1()
    x_dcin.wait_recv()
    rg[...] = (cot[...].astype(F32) + 0.125 * mm(m_n[...], dcinb[...].reshape(1024, W))).astype(BF)

    dz = norm_back(rg[...].astype(F32), yn[...].astype(F32), rsn[...])
    dh = (mm_nt(dz, fw[1536:1792]) * gn[...].astype(F32)).astype(BF)
    dnp[...] = rg[...].astype(F32) + mm_nt(dh, fw[1024:1280])
    dsm[...] = mm_nt(dh, fw[1280:1536]).astype(BF)
    put(middle.s, halves, 256, mm_tn(nodes[...], dh))
    put(middle.s, halves, 512, mm_tn(summed[...], dh))
    put(middle.s, halves, 768, mm_tn(an[...], dz))
    middle.stage0()
    early.stage2()

    s_s[...] = jnp.zeros_like(s_s)
    g_ae[...] = jnp.zeros_like(g_ae)
    g_b[...] = jnp.zeros_like(g_b)

    def edge_backward(t, c):
        base = pl.multiple_of(t * 512, 512)
        nbase = pl.multiple_of(t * 128, 128)
        cols = []
        for j in range(4):
            rrow = rcv[pl.ds(4 * t + j, 1), :] - 128 * t
            cols.append(hot((column(rrow) == lane) & (sub + 128 * j < count)))

        def turned(b):
            return jnp.concatenate([oh[t, b, 128 * j:128 * j + 128, :] for j in range(4)], axis=1)

        dmsg = mm(jnp.concatenate(cols, axis=0), dsm[pl.ds(nbase, 128), :])
        dz = norm_back(dmsg, yv[pl.ds(base, 512), :].astype(F32), rsv[pl.ds(base, 512), :])
        dh = (mm_nt(dz, fw[768:1024]) * gpr[pl.ds(base, 512), :].astype(F32)).astype(BF)
        gpr[pl.ds(base, 512), :] = dh
        g_b[...] += mm_tn(act[pl.ds(base, 512), :], dz)
        g_ae[...] += mm_tn(edges[pl.ds(base, 512), :], dh)
        for q in range(3):
            part = jnp.concatenate([turned(4 * q + b) for b in range(4)], axis=0)
            s_s[512 * q:512 * q + 512, :] += mm(part, dh)
        s_r[pl.ds(nbase, 128), :] = mm(turned(12), dh).astype(BF)
        return c

    lax.fori_loop(0, 2, edge_backward, 0)
    early.stage3()
    middle.stage1()
    lax.fori_loop(2, TILES, edge_backward, 0)

    put(late.sa, single, 0, g_b[...])
    late.a1.start()
    ss = s_s[...].astype(BF)
    g_as = mm_tn(nodes[...], ss[0:1024]) + mm_tn(hin[...].reshape(512, W), ss[1024:1536])
    put(late.sb, single, 0, g_ae[...])
    put(late.sb, single, 256, g_as)
    put(late.sb, single, 512, mm_tn(nodes[...], s_r[...]))
    late.b1.start()
    hret[...] = mm_nt(ss[1024:1536], fw[256:512]).astype(BF).reshape(16, 32, W)
    x_ret.start()
    middle.stage2()
    early.stage4()

    def edge_out(t, c):
        rows = pl.ds(pl.multiple_of(t * 512, 512), 512)
        edge_grad[rows, :] = mm_nt(gpr[rows, :], fw[0:256]).astype(BF)
        return c

    lax.fori_loop(0, TILES, edge_out, 0)
    st_edge = pltpu.make_async_copy(edge_grad, edge_grad_h, osem.at[1])
    st_edge.start()
    late.stage2()
    middle.stage3()
    own = dnp[...] + mm_nt(ss[0:1024], fw[256:512]) + mm_nt(s_r[...], fw[512:768])
    x_ret.wait_recv()
    node_grad[...] = (own + mm_tn(ohh[...], hrin[...].reshape(512, W))).astype(BF)
    st_node = pltpu.make_async_copy(node_grad, node_grad_h, osem.at[2])
    st_node.start()
    late.stage3()
    middle.stage4()
    early.finish()
    stores = [st_fine, st_edge, st_node]

    def store(ref, at):
        rows = ref.shape[0]
        copy = pltpu.make_async_copy(ref, grads_h.at[pl.ds(at, rows)], osem.at[len(stores)])
        copy.start()
        stores.append(copy)

    def store_blocks(ref, at):
        rows = ref.shape[-2]
        if len(ref.shape) == 4:
            for h in range(2):
                store_blocks(ref.at[h], at + h * DOM * rows)
        else:
            n = ref.shape[0]
            flat = staged.at[pl.ds(at, n * rows)]
            flat[...] = ref[...].reshape(n * rows, W)
            store(flat, at)

    store_blocks(early.o, 0)
    middle.finish()
    store_blocks(middle.o, 1536)
    late.finish()
    store_blocks(late.oa, 2560)
    store_blocks(late.ob, 2816)
    for c in stores:
        c.wait()
    for x in links.all:
        x.wait_send()


def place(
    fine_h, node_h, edge_h, grads_h, fine_o, node_o, edge_o, fw_o, cw_o,
    fine, node, edge, grads, fwg, cwg, lsem, ssem,
):
    half = edge.shape[0] // 2
    parts = [(grads_h, grads, None), (fine_h, fine, fine_o), (node_h, node, node_o)]
    for i in range(2):
        rows = pl.ds(half * i, half)
        parts.append((edge_h.at[rows], edge.at[rows], edge_o.at[rows]))
    loads = [pltpu.make_async_copy(a, b, lsem.at[i]) for i, (a, b, c) in enumerate(parts)]
    moves = [pltpu.make_async_copy(b, c, ssem.at[i]) for i, (a, b, c) in enumerate(parts) if i > 0]
    for c in loads:
        c.start()
    for c, m in zip(loads[1:], moves):
        c.wait()
        m.start()
    loads[0].wait()

    def scaled(at, rows, scale):
        return grads[at:at + rows].astype(F32) * scale

    cwg[0:256] = scaled(0, 256, COARSE_SCALE)
    cwg[256:768] = scaled(1280, 512, COARSE_SCALE)
    cwg[768:1792] = scaled(256, 1024, COARSE_SCALE)
    fwg[0:768] = scaled(2816, 768, FINE_SCALE)
    fwg[768:1024] = scaled(2560, 256, FINE_SCALE)
    fwg[1024:1792] = scaled(1792, 768, FINE_SCALE)
    last = [pltpu.make_async_copy(fwg, fw_o, ssem.at[5]), pltpu.make_async_copy(cwg, cw_o, ssem.at[6])]
    for c in last:
        c.start()
    for c in moves + last:
        c.wait()


def body(
    nodes, edges, senders, receivers, edge_count, halo_rows, aggregates,
    coarse_edges, coarse_senders, coarse_receivers, cotangent, fine_weights, coarse_weights,
):
    vm = pl.BlockSpec(memory_space=pltpu.VMEM)
    hbm = pl.BlockSpec(memory_space=pl.ANY)
    V = pltpu.VMEM
    scratch = [
        V((1024, W), BF),
        V((4096, W), BF),
        V((1024, W), BF),
        V((1792, W), BF),
        V((1792, W), BF),
        V((512, W), BF),
        V((1024, W), BF),
        V((1024, W), BF),
        V((16, 128), jnp.int32),
        V((8, 128), jnp.int32),
        V((512, 1024), BF),
        V((16, 32, W), BF),
        V((16, 32, W), BF),
        V((2, 512, 1024), BF),
        V((1024, 1024), BF),
        V((8, 13, 512, 128), BF),
        V((1920, W), BF),
        V((1024, W), BF),
        V((4096, W), BF),
        V((4096, W), BF),
        V((4096, W), BF),
        V((4096, 1), F32),
        V((1024, W), BF),
        V((1024, W), BF),
        V((1024, W), BF),
        V((1024, W), BF),
        V((1024, 1), F32),
        V((1024, W), BF),
        V((8, 128, W), BF),
        V((512, 1408), BF),
        V((1408, W), BF),
        V((512, W), BF),
        V((512, W), BF),
        V((512, W), BF),
        V((512, 1), F32),
        V((8, 128, W), BF),
        V((8, 128, W), BF),
        V((1024, W), BF),
        V((1024, W), F32),
        V((1024, W), BF),
        V((1536, W), F32),
        V((1024, W), BF),
        V((256, W), F32),
        V((256, W), F32),
        V((16, 32, W), BF),
        V((16, 32, W), BF),
        pltpu.SemaphoreType.DMA((256,)),
        pltpu.SemaphoreType.DMA((256,)),
        pltpu.SemaphoreType.DMA((6,)),
        pltpu.SemaphoreType.DMA((12,)),
    ]
    for _ in range(3):
        scratch += [V((2, YS, 128, W), BF), V((YS, 128, W), BF), V((YS, 128, W), BF), V((YS, 128, W), BF)]
    for rows in (48, 32):
        scratch += [V((2, DOM, rows, W), BF), V((DOM, rows, W), BF), V((DOM, rows, W), BF),
                    V((DOM, rows, W), BF), V((YS, rows, W), BF), V((2, DOM, rows, W), BF)]
    scratch += [V((GRP, 32, W), BF), V((GRP, 32, W), BF), V((DOM, 32, W), BF), V((GRP, 32, W), BF),
                V((DOM, 48, W), BF), V((DOM, 48, W), BF), V((GRP, 48, W), BF), V((DOM, 48, W), BF)]
    shape = jax.ShapeDtypeStruct
    fine_out, node_grad, edge_grad, grads = pl.pallas_call(
        kernel,
        out_shape=(shape((1024, W), BF), shape((1024, W), BF), shape((4096, W), BF), shape((3584, W), BF)),
        in_specs=[hbm, hbm, vm, vm, pl.BlockSpec(memory_space=pltpu.SMEM), vm, vm,
                  hbm, vm, vm, hbm, hbm, hbm],
        out_specs=(hbm,) * 4,
        scratch_shapes=scratch,
        compiler_params=pltpu.CompilerParams(
            collective_id=0, has_side_effects=True, vmem_limit_bytes=62 * 1024 * 1024
        ),
    )(
        nodes, edges, senders.reshape(32, 128), receivers.reshape(32, 128), edge_count,
        halo_rows.reshape(16, 32), aggregates.reshape(8, 128), coarse_edges,
        coarse_senders.reshape(32, 128), coarse_receivers.reshape(32, 128), cotangent,
        fine_weights, coarse_weights,
    )
    return pl.pallas_call(
        place,
        out_shape=(shape((1024, W), BF), shape((1024, W), BF), shape((4096, W), BF),
                   shape((1792, W), F32), shape((1792, W), F32)),
        in_specs=[hbm] * 4,
        out_specs=(hbm,) * 5,
        scratch_shapes=[V((1024, W), BF), V((1024, W), BF), V((4096, W), BF), V((3584, W), BF), V((1792, W), F32),
                        V((1792, W), F32), pltpu.SemaphoreType.DMA((5,)), pltpu.SemaphoreType.DMA((7,))],
        compiler_params=pltpu.CompilerParams(vmem_limit_bytes=62 * 1024 * 1024),
    )(fine_out, node_grad, edge_grad, grads)


def solution(mesh):
    both = ("dom", "grp")
    placed = (
        P(both, None), P(both, None), P(both), P(both), P(both), P(both, None, None), P(both),
        P("dom", None, None), P("dom", None), P("dom", None), P(both, None), P(), P(),
    )
    return jax.shard_map(
        body, mesh=mesh, in_specs=placed,
        out_specs=(P(both, None), P(both, None), P(both, None), P(), P()),
        check_vma=False,
    )
```

time: 138 us -> 112 us (0.81)
  Pallas kernels: 127 us -> 110 us
  local copies, waits for them, and re-layouts: 9.53 us -> 0 us
    pallas_call x1 -> x2, Pallas kernels: 127 us -> 110 us  [the longest x1 106 us: body(): pl.pallas_call(kernel, out_shape=(shape((1024, W), BF), shape((1024, W),...]
    unnamed x11 -> x0, local copies, waits for them, and re-layouts: 9.53 us -> none
where the time goes in v2:
time: 112 us
  Pallas kernels  110 us (98%)
  between operations  1.45 us (1%)
    pallas_call x1, Pallas kernels, body(): pl.pallas_call(kernel, out_shape=(shape((1024, W), BF), shape((1024, W),...  106 us
    pallas_call x1, Pallas kernels, body(): pl.pallas_call(place, out_shape=(shape((1024, W), BF), shape((1024, W), B...  4.72 us

profile of v2, /device:TPU:1, one launch (start us, length us, event | category | flops | bytes accessed | tf_op | source)
XLA Modules:
  0.0 111.9 jit_solution(9304303134441006711)
XLA Ops:
  1.3 105.7 %shard_map.164 = (bf16[1024,256]{1,0:T(8,128)(2,1)}, bf16[1024,256]{1,0:T(8,128)(2,1)}, bf16[4096,256]{1,0:T(8,128)(2,1)}, bf16[3584,256]{1,0:T(8,128)(2,1)}) custom-call(bf16[1024,256]{1,0:T(8,128)(2,1)} %nodes_h.1, bf16[4096,256]{1,0:T(8,128)(2,1)} %edges_h.1, s32[32,128]{1,0:T(8,128)} %bitcast.6, s32[32,128]{1,0:T(8,128)} %bitcast.7, s32[1]{0:T(128)S(6)} %copy.18.cnt, ...), custom_call_target="tpu_custom_call" | custom-call | tf_op jit(solution)/shard_map/pallas_call | solution.py:709
  107.0 4.7 %shard_map.165 = (bf16[1024,256]{1,0:T(8,128)(2,1)}, bf16[1024,256]{1,0:T(8,128)(2,1)}, bf16[4096,256]{1,0:T(8,128)(2,1)}, f32[1792,256]{1,0:T(8,128)}, f32[1792,256]{1,0:T(8,128)}) custom-call(bf16[1024,256]{1,0:T(8,128)(2,1)} %get-tuple-element.9.fine_h, bf16[1024,256]{1,0:T(8,128)(2,1)} %get-tuple-element.10.node_h, ...), custom_call_target="tpu_custom_call" | custom-call | tf_op jit(solution)/shard_map/pallas_call | solution.py:725

commit v3 on v2

--- a/solution.py
+++ b/solution.py
@@ -13,6 +13,7 @@
 GRP = 8
 TILES = 8
 YS = 4
+BIG = 2048
 FINE_SCALE = 524288 ** (-0.5)
 COARSE_SCALE = 65536 ** (-0.5)
 
@@ -35,6 +36,10 @@
 
 def hot(mask):
     return jnp.where(mask, 1.0, 0.0).astype(BF)
+
+
+def hot16(mask):
+    return jnp.where(mask, jnp.ones(mask.shape, BF), jnp.zeros(mask.shape, BF))
 
 
 def column(row):
@@ -57,6 +62,25 @@
     first = jnp.mean(dy, axis=-1, keepdims=True)
     second = jnp.mean(dy * y, axis=-1, keepdims=True)
     return (rs * (dy - first - y * second)).astype(BF)
+
+
+def norm_back_centred(dy, y, rs):
+    second = jnp.mean(dy * y, axis=-1, keepdims=True)
+    return (rs * (dy - y * second)).astype(BF)
+
+
+def turn(ref, rows, count):
+    def step(i, c):
+        block = pl.ds(pl.multiple_of(rows + 256 * i, 256), 256)
+        ref[block, :] = ref[block, :].T
+        return c
+
+    lax.fori_loop(0, count, step, 0)
+
+
+def mm_turned(ref, rows, count, b):
+    left = [ref[rows + 256 * i:rows + 256 * i + 256, :] for i in range(count)]
+    return mm(jnp.concatenate(left, axis=1), b)
 
 
 class Links:
@@ -106,7 +130,7 @@
             act(self.copy(k))
             return carry
 
-        if self.count <= YS:
+        if self.count <= DOM:
             for k in range(1, self.count):
                 step(k, 0)
         else:
@@ -169,7 +193,7 @@
             x.wait_recv()
 
 
-class EarlySum:
+class AllSum:
     def __init__(self, links, s, m, t, r, v, o):
         self.links, self.s, self.m, self.t, self.r, self.v, self.o = links, s, m, t, r, v, o
         d, y, core = links.d, links.y, links.core
@@ -205,42 +229,6 @@
         self.x4.wait_recv()
 
 
-class LateSum:
-    def __init__(self, links, sa, ra, va, oa, sb, rb, vb, ob):
-        self.links = links
-        self.sa, self.ra, self.va, self.oa = sa, ra, va, oa
-        self.sb, self.rb, self.vb, self.ob = sb, rb, vb, ob
-        d, g = links.d, links.g
-        self.a1 = links.exchange("grp", lambda p: sa.at[p], lambda k: ra.at[k])
-        self.b1 = links.exchange("dom", lambda p: sb.at[p], lambda k: rb.at[k])
-        self.a2 = links.exchange("dom", lambda p: va.at[d], lambda k: va.at[d])
-        self.b2 = links.exchange("grp", lambda p: vb.at[g], lambda k: vb.at[g])
-        self.a3 = links.exchange("grp", lambda p: oa.at[g], lambda k: oa.at[g])
-        self.b3 = links.exchange("dom", lambda p: ob.at[d], lambda k: ob.at[d])
-
-    def stage2(self):
-        d, g = self.links.d, self.links.g
-        self.a1.wait_recv()
-        self.va[d] = total_of(self.sa[g], self.ra, range(1, GRP)).astype(BF)
-        self.a2.start()
-        self.b1.wait_recv()
-        self.vb[g] = total_of(self.sb[d], self.rb, range(1, DOM)).astype(BF)
-        self.b2.start()
-
-    def stage3(self):
-        d, g = self.links.d, self.links.g
-        self.b2.wait_recv()
-        self.ob[d] = total_of(self.vb[0], self.vb, range(1, GRP)).astype(BF)
-        self.b3.start()
-        self.a2.wait_recv()
-        self.oa[g] = total_of(self.va[0], self.va, range(1, DOM)).astype(BF)
-        self.a3.start()
-
-    def finish(self):
-        self.a3.wait_recv()
-        self.b3.wait_recv()
-
-
 def put(ref, lead, at, value):
     value = value.astype(BF)
     rows, pos = ref.shape[-2], 0
@@ -255,20 +243,18 @@
     return (block // DOM, block % DOM)
 
 
-def single(block):
-    return (block,)
-
-
 def kernel(
     nodes_h, edges_h, snd, rcv, cnt, halo, agg, cedges_h, csnd, crcv, cot_h, fw_h, cw_h,
     fine_out_h, node_grad_h, edge_grad_h, grads_h, *s
 ):
-    (nodes, edges, cot, fw, cw, ce, fine_out, node_grad,
-     hpad, hr, ohh, outg, hin, m_t, m_n, oh, wcat, p_r, act, gpr, yv, rsv, summed,
+    (nodes, edges, cot, fw, cw, ce,
+     hpad, hr, ohh, outg, hin, m_t, oh, ohr, wcat, p_r, act, gpr, yv, rsv, summed,
      an, gn, yn, rsn, refined, cinb, cx, cwc, cact, cgp, cy, crs, coutb,
-     dcinb, rg, dnp, dsm, s_s, s_r, g_ae, g_b, hret, hrin, ssem, rsem, isem, osem) = s[:50]
-    rest = list(s[50:])
-    edge_grad, staged = yv, act
+     dcinb, rg, work, dsm, s_r, hret, hrin, ssem, rsem, isem, osem) = s[:45]
+    rest = list(s[45:])
+    edge_grad, staged, fine_out, node_grad = yv, act, refined, rg
+    s_s, dnp = work.at[0:1536], work.at[1536:2560]
+    g_ae, g_b = work.at[2560:2816], work.at[2816:3072]
 
     def take(n):
         out = rest[:n]
@@ -310,12 +296,14 @@
     x_cin = GroupGather(links, cinb)
     x_cout = GroupGather(links, coutb)
     x_dcin = GroupGather(links, dcinb)
-    early = EarlySum(links, *take(6))
-    middle = EarlySum(links, *take(6))
-    late = LateSum(links, *take(8))
+    early = AllSum(links, *take(6))
+    middle = AllSum(links, *take(6))
+    late = AllSum(links, *take(6))
 
     lane = iota((128, 128), 1)
     sub = iota((128, 128), 0)
+    lane16 = lane.astype(jnp.int16)
+    sub16 = sub.astype(jnp.int16)
 
     hpad[...] = jnp.zeros_like(hpad)
     hpad[:, 0:32] = halo[...]
@@ -338,11 +326,9 @@
 
     def member(j, c):
         row = agg[pl.ds(j, 1), :]
-        col = column(row)
         at = pl.multiple_of(j * 128, 128)
         for b in range(8):
             m_t[b % 2, 128 * (b // 2):128 * (b // 2) + 128, pl.ds(at, 128)] = hot(sub + 128 * b == row)
-            m_n[pl.ds(at, 128), 128 * b:128 * b + 128] = hot(col == lane + 128 * b)
         return c
 
     lax.fori_loop(0, 8, member, 0)
@@ -359,54 +345,64 @@
     def edge_hot(t, c):
         for j in range(4):
             rows = slice(128 * j, 128 * j + 128)
-            scol = column(snd[pl.ds(4 * t + j, 1), :])
+            scol = column(snd[pl.ds(4 * t + j, 1), :]).astype(jnp.int16)
             rcol = column(rcv[pl.ds(4 * t + j, 1), :] - 128 * t)
             for b in range(12):
-                oh[t, b, rows, :] = hot(scol == lane + 128 * b)
-            oh[t, 12, rows, :] = hot((rcol == lane) & (sub + 128 * j < count))
-        return c
-
-    lax.fori_loop(0, TILES, edge_hot, 0)
+                oh[t, b, rows, :] = hot16(scol == lane16 + jnp.int16(128 * b))
+            ohr[t, rows, :] = hot((rcol == lane) & (sub + 128 * j < count))
+        return c
+
+    lax.fori_loop(0, TILES, edge_hot, 0, unroll=2)
     pro.pair()
     ld_edges.wait()
+
+    def edge_local(i, c):
+        rows = pl.ds(pl.multiple_of(i * BIG, BIG), BIG)
+        tiles = [i * (BIG // 512) + q for q in range(BIG // 512)]
+        far = [jnp.concatenate([oh[t, b] for b in range(8)], axis=1) for t in tiles]
+        near = [mm(ohr[t], p_r[pl.ds(pl.multiple_of(t * 128, 128), 128), :]) for t in tiles]
+        joined = jnp.concatenate([edges[rows, :], jnp.concatenate(far, axis=0)], axis=1)
+        work[rows, :] = mm(joined, wcat[0:1280]) + jnp.concatenate(near, axis=0)
+        return c
+
+    lax.fori_loop(0, 4096 // BIG, edge_local, 0)
     x_halo.wait_recv()
     wcat[1280:1792] = mm(hin[...].reshape(512, W), fw[256:512]).astype(BF)
 
-    def edge_forward(t, c):
-        base = pl.multiple_of(t * 512, 512)
-        nbase = pl.multiple_of(t * 128, 128)
+    def edge_forward(i, c):
+        rows = pl.ds(pl.multiple_of(i * BIG, BIG), BIG)
+        tiles = [i * (BIG // 512) + q for q in range(BIG // 512)]
+        far = [jnp.concatenate([oh[t, b] for b in range(8, 12)], axis=1) for t in tiles]
+        a, gp = silu_parts(work[rows, :] + mm(jnp.concatenate(far, axis=0), wcat[1280:1792]))
+        act[rows, :] = a
+        gpr[rows, :] = gp
+        y, rs = norm(mm(a, fw[768:1024]))
+        yv[rows, :] = y.astype(BF)
+        rsv[rows, :] = rs
+        return c
+
+    def edge_sum(t, c):
         back = []
         for j in range(4):
             rrow = rcv[pl.ds(4 * t + j, 1), :] - 128 * t
             back.append(hot((rrow == sub) & (lane + 128 * j < count)))
-        wcat[1792:1920] = p_r[pl.ds(nbase, 128), :]
-        joined = jnp.concatenate([edges[pl.ds(base, 512), :]] + [oh[t, b] for b in range(13)], axis=1)
-        h = mm(joined, wcat[...])
-        a, gp = silu_parts(h)
-        act[pl.ds(base, 512), :] = a
-        gpr[pl.ds(base, 512), :] = gp
-        y, rs = norm(mm(a, fw[768:1024]))
-        y = y.astype(BF)
-        yv[pl.ds(base, 512), :] = y
-        rsv[pl.ds(base, 512), :] = rs
-        summed[pl.ds(nbase, 128), :] = mm(jnp.concatenate(back, axis=1), y).astype(BF)
-        return c
-
-    lax.fori_loop(0, TILES, edge_forward, 0)
-
-    def node_forward(t, c):
         rows = pl.ds(pl.multiple_of(t * 512, 512), 512)
-        h = mm(nodes[rows, :], fw[1024:1280]) + mm(summed[rows, :], fw[1280:1536])
-        a, gp = silu_parts(h)
-        an[rows, :] = a
-        gn[rows, :] = gp
-        y, rs = norm(mm(a, fw[1536:1792]))
-        yn[rows, :] = y.astype(BF)
-        rsn[rows, :] = rs
-        refined[rows, :] = (nodes[rows, :].astype(F32) + y).astype(BF)
-        return c
-
-    lax.fori_loop(0, 2, node_forward, 0)
+        summed[pl.ds(pl.multiple_of(t * 128, 128), 128), :] = mm(
+            jnp.concatenate(back, axis=1), yv[rows, :]).astype(BF)
+        return c
+
+    lax.fori_loop(0, 4096 // BIG, edge_forward, 0)
+    lax.fori_loop(0, TILES, edge_sum, 0, unroll=TILES)
+
+    a, gp = silu_parts(mm(nodes[...], fw[1024:1280]) + mm(summed[...], fw[1280:1536]))
+    an[...] = a
+    gn[...] = gp
+    ynode, rs = norm(mm(a, fw[1536:1792]))
+    yn[...] = ynode.astype(BF)
+    rsn[...] = rs
+    refined[...] = (nodes[...].astype(F32) + ynode).astype(BF)
+    hin_t = p_r
+    hin_t[0:512] = hin[...].reshape(512, W)
 
     res.s[1 - core] = (mm(m_t[1 - core], refined[...]) * 0.125).astype(BF).reshape(YS, 128, W)
     res.first.start()
@@ -416,16 +412,21 @@
     def edge_hot_back(t, c):
         for j in range(4):
             rows = slice(128 * j, 128 * j + 128)
-            srow = snd[pl.ds(4 * t + j, 1), :]
+            srow = jnp.broadcast_to(snd[pl.ds(4 * t + j, 1), :], (128, 128)).astype(jnp.int16)
             rrow = rcv[pl.ds(4 * t + j, 1), :] - 128 * t
             for b in range(12):
-                oh[t, b, rows, :] = hot(srow == sub + 128 * b)
+                oh[t, b, rows, :] = hot16(srow == sub16 + jnp.int16(128 * b))
             oh[t, 12, rows, :] = hot((rrow == sub) & (lane + 128 * j < count))
+        return c
+
+    def member_back(j, c):
+        col = column(agg[pl.ds(j, 1), :])
+        for b in range(8):
+            m_t[j // 4, pl.ds(pl.multiple_of(lax.rem(j, 4) * 128, 128), 128), 128 * b:128 * b + 128] = hot(col == lane + 128 * b)
         return c
 
     ld_ce.wait()
     ld_cw.wait()
-    cx[:, 0:256] = ce[...]
     cback = []
     for j in range(4):
         srow = csnd[pl.ds(4 * g + j, 1), :]
@@ -433,13 +434,17 @@
         scol = column(srow)
         rcol = column(rrow)
         for b in range(8):
-            cx[128 * j:128 * j + 128, 256 + 128 * b:384 + 128 * b] = hot(scol == lane + 128 * b)
-        cx[128 * j:128 * j + 128, 1280:1408] = hot(rcol == lane)
+            m_t[0, 128 * j:128 * j + 128, 128 * b:128 * b + 128] = hot(scol == lane + 128 * b)
+        cx[128 * j:128 * j + 128, :] = hot(rcol == lane)
         cback.append(hot(rrow == sub))
     cback = jnp.concatenate(cback, axis=1)
     cwc[0:256] = cw[0:256]
     pg = pro.result().astype(BF).astype(F32)
     lax.fori_loop(0, 3, edge_hot_back, 0)
+    turn(nodes, 0, 4)
+    turn(summed, 0, 4)
+    turn(an, 0, 4)
+    turn(hin_t, 0, 2)
     cin = res.result().astype(BF)
     cinb[g] = cin
     x_cin.start()
@@ -447,7 +452,7 @@
     lax.fori_loop(3, TILES, edge_hot_back, 0)
     x_cin.wait_recv()
     cwc[256:1280] = mm(cinb[...].reshape(1024, W), cw[256:512]).astype(BF)
-    ca, cg = silu_parts(mm(cx[...], cwc[...]))
+    ca, cg = silu_parts(mm(jnp.concatenate([ce[...], m_t[0], cx[...]], axis=1), cwc[...]))
     cact[...] = ca
     cgp[...] = cg
     cyn, rs = norm(mm(ca, cw[768:1024]))
@@ -463,7 +468,7 @@
     cndh = (mm_nt(cndz, cw[1536:1792]) * cng.astype(F32)).astype(BF)
     dcin_part = pg + mm_nt(cndh, cw[1024:1280])
     dcsum = mm_nt(cndh, cw[1280:1536]).astype(BF)
-    cdz = norm_back(mm(cx[:, 1280:1408], dcsum), cy[...].astype(F32), crs[...])
+    cdz = norm_back(mm(cx[...], dcsum), cy[...].astype(F32), crs[...])
     cdh = (mm_nt(cdz, cw[768:1024]) * cgp[...].astype(F32)).astype(BF)
 
     def sender_sum(half):
@@ -487,6 +492,8 @@
     put(early.s, halves, 1024, mm_tn(cna, cndz))
     put(middle.s, halves, 0, mm_tn(cin, s_cr))
     dcin_part = dcin_part + mm_nt(s_cr, cw[512:768])
+    lax.fori_loop(0, 8, member_back, 0)
+    turn(edges, 0, 8)
     s_tot = sen.result().astype(BF)
     dcinb[g] = (dcin_part + mm_nt(s_tot, cw[256:512])).astype(BF)
     x_dcin.start()
@@ -494,20 +501,23 @@
     early.stage0()
 
     x_cout.wait_recv()
-    fine_out[...] = (refined[...].astype(F32) + mm(m_n[...], coutb[...].reshape(1024, W))).astype(BF)
+    fine_out[...] = (refined[...].astype(F32) + mm(m_t[...].reshape(1024, 1024), coutb[...].reshape(1024, W))).astype(BF)
     st_fine = pltpu.make_async_copy(fine_out, fine_out_h, osem.at[0])
     st_fine.start()
     early.stage1()
+    turn(edges, 2048, 8)
+    turn(act, 0, 16)
     x_dcin.wait_recv()
-    rg[...] = (cot[...].astype(F32) + 0.125 * mm(m_n[...], dcinb[...].reshape(1024, W))).astype(BF)
+    rg[...] = (cot[...].astype(F32) + 0.125 * mm(m_t[...].reshape(1024, 1024), dcinb[...].reshape(1024, W))).astype(BF)
 
     dz = norm_back(rg[...].astype(F32), yn[...].astype(F32), rsn[...])
     dh = (mm_nt(dz, fw[1536:1792]) * gn[...].astype(F32)).astype(BF)
     dnp[...] = rg[...].astype(F32) + mm_nt(dh, fw[1024:1280])
-    dsm[...] = mm_nt(dh, fw[1280:1536]).astype(BF)
-    put(middle.s, halves, 256, mm_tn(nodes[...], dh))
-    put(middle.s, halves, 512, mm_tn(summed[...], dh))
-    put(middle.s, halves, 768, mm_tn(an[...], dz))
+    dsum = mm_nt(dh, fw[1280:1536]).astype(BF).astype(F32)
+    dsm[...] = (dsum - jnp.mean(dsum, axis=-1, keepdims=True)).astype(BF)
+    put(middle.s, halves, 256, mm_turned(nodes, 0, 4, dh))
+    put(middle.s, halves, 512, mm_turned(summed, 0, 4, dh))
+    put(middle.s, halves, 768, mm_turned(an, 0, 4, dz))
     middle.stage0()
     early.stage2()
 
@@ -515,64 +525,57 @@
     g_ae[...] = jnp.zeros_like(g_ae)
     g_b[...] = jnp.zeros_like(g_b)
 
-    def edge_backward(t, c):
-        base = pl.multiple_of(t * 512, 512)
-        nbase = pl.multiple_of(t * 128, 128)
-        cols = []
-        for j in range(4):
-            rrow = rcv[pl.ds(4 * t + j, 1), :] - 128 * t
-            cols.append(hot((column(rrow) == lane) & (sub + 128 * j < count)))
-
-        def turned(b):
+    def edge_backward(i):
+        base = i * BIG
+        rows = pl.ds(base, BIG)
+        tiles = [i * (BIG // 512) + q for q in range(BIG // 512)]
+        dmsg = jnp.concatenate([mm(ohr[t], dsm[128 * t:128 * t + 128, :]) for t in tiles], axis=0)
+        dz = norm_back_centred(dmsg, yv[rows, :].astype(F32), rsv[rows, :])
+        dh = (mm_nt(dz, fw[768:1024]) * gpr[rows, :].astype(F32)).astype(BF)
+        gpr[rows, :] = dh
+        g_b[...] += mm_turned(act, base, BIG // 256, dz)
+        g_ae[...] += mm_turned(edges, base, BIG // 256, dh)
+
+        def turned(t, b):
             return jnp.concatenate([oh[t, b, 128 * j:128 * j + 128, :] for j in range(4)], axis=1)
 
-        dmsg = mm(jnp.concatenate(cols, axis=0), dsm[pl.ds(nbase, 128), :])
-        dz = norm_back(dmsg, yv[pl.ds(base, 512), :].astype(F32), rsv[pl.ds(base, 512), :])
-        dh = (mm_nt(dz, fw[768:1024]) * gpr[pl.ds(base, 512), :].astype(F32)).astype(BF)
-        gpr[pl.ds(base, 512), :] = dh
-        g_b[...] += mm_tn(act[pl.ds(base, 512), :], dz)
-        g_ae[...] += mm_tn(edges[pl.ds(base, 512), :], dh)
         for q in range(3):
-            part = jnp.concatenate([turned(4 * q + b) for b in range(4)], axis=0)
-            s_s[512 * q:512 * q + 512, :] += mm(part, dh)
-        s_r[pl.ds(nbase, 128), :] = mm(turned(12), dh).astype(BF)
-        return c
-
-    lax.fori_loop(0, 2, edge_backward, 0)
-    early.stage3()
-    middle.stage1()
-    lax.fori_loop(2, TILES, edge_backward, 0)
-
-    put(late.sa, single, 0, g_b[...])
-    late.a1.start()
+            part = [jnp.concatenate([turned(t, 4 * q + b) for t in tiles], axis=1) for b in range(4)]
+            s_s[512 * q:512 * q + 512, :] += mm(jnp.concatenate(part, axis=0), dh)
+        for q, t in enumerate(tiles):
+            s_r[128 * t:128 * t + 128, :] = mm(turned(t, 12), dh[512 * q:512 * q + 512]).astype(BF)
+
+    for i in range(4096 // BIG):
+        if i == 4096 // BIG // 2:
+            early.stage3()
+            middle.stage1()
+        edge_backward(i)
+
+    put(late.s, halves, 0, g_ae[...])
+    put(late.s, halves, 256, g_b[...])
     ss = s_s[...].astype(BF)
-    g_as = mm_tn(nodes[...], ss[0:1024]) + mm_tn(hin[...].reshape(512, W), ss[1024:1536])
-    put(late.sb, single, 0, g_ae[...])
-    put(late.sb, single, 256, g_as)
-    put(late.sb, single, 512, mm_tn(nodes[...], s_r[...]))
-    late.b1.start()
+    put(late.s, halves, 512, mm_turned(nodes, 0, 4, ss[0:1024]) + mm_turned(hin_t, 0, 2, ss[1024:1536]))
+    put(late.s, halves, 768, mm_turned(nodes, 0, 4, s_r[...]))
+    late.stage0()
     hret[...] = mm_nt(ss[1024:1536], fw[256:512]).astype(BF).reshape(16, 32, W)
+    late.stage1()
     x_ret.start()
     middle.stage2()
     early.stage4()
 
-    def edge_out(t, c):
-        rows = pl.ds(pl.multiple_of(t * 512, 512), 512)
+    for i in range(4096 // BIG):
+        rows = pl.ds(i * BIG, BIG)
         edge_grad[rows, :] = mm_nt(gpr[rows, :], fw[0:256]).astype(BF)
-        return c
-
-    lax.fori_loop(0, TILES, edge_out, 0)
     st_edge = pltpu.make_async_copy(edge_grad, edge_grad_h, osem.at[1])
     st_edge.start()
+    own = dnp[...] + mm_nt(ss[0:1024], fw[256:512]) + mm_nt(s_r[...], fw[512:768])
     late.stage2()
     middle.stage3()
-    own = dnp[...] + mm_nt(ss[0:1024], fw[256:512]) + mm_nt(s_r[...], fw[512:768])
     x_ret.wait_recv()
     node_grad[...] = (own + mm_tn(ohh[...], hrin[...].reshape(512, W))).astype(BF)
     st_node = pltpu.make_async_copy(node_grad, node_grad_h, osem.at[2])
     st_node.start()
     late.stage3()
-    middle.stage4()
     early.finish()
     stores = [st_fine, st_edge, st_node]
 
@@ -594,11 +597,12 @@
             store(flat, at)
 
     store_blocks(early.o, 0)
+    middle.stage4()
+    late.stage4()
     middle.finish()
     store_blocks(middle.o, 1536)
     late.finish()
-    store_blocks(late.oa, 2560)
-    store_blocks(late.ob, 2816)
+    store_blocks(late.o, 2560)
     for c in stores:
         c.wait()
     for x in links.all:
@@ -629,8 +633,9 @@
     cwg[0:256] = scaled(0, 256, COARSE_SCALE)
     cwg[256:768] = scaled(1280, 512, COARSE_SCALE)
     cwg[768:1792] = scaled(256, 1024, COARSE_SCALE)
-    fwg[0:768] = scaled(2816, 768, FINE_SCALE)
-    fwg[768:1024] = scaled(2560, 256, FINE_SCALE)
+    fwg[0:256] = scaled(2560, 256, FINE_SCALE)
+    fwg[256:768] = scaled(3072, 512, FINE_SCALE)
+    fwg[768:1024] = scaled(2816, 256, FINE_SCALE)
     fwg[1024:1792] = scaled(1792, 768, FINE_SCALE)
     last = [pltpu.make_async_copy(fwg, fw_o, ssem.at[5]), pltpu.make_async_copy(cwg, cw_o, ssem.at[6])]
     for c in last:
@@ -653,17 +658,15 @@
         V((1792, W), BF),
         V((1792, W), BF),
         V((512, W), BF),
-        V((1024, W), BF),
-        V((1024, W), BF),
         V((16, 128), jnp.int32),
         V((8, 128), jnp.int32),
         V((512, 1024), BF),
         V((16, 32, W), BF),
         V((16, 32, W), BF),
         V((2, 512, 1024), BF),
-        V((1024, 1024), BF),
         V((8, 13, 512, 128), BF),
-        V((1920, W), BF),
+        V((8, 512, 128), BF),
+        V((1792, W), BF),
         V((1024, W), BF),
         V((4096, W), BF),
         V((4096, W), BF),
@@ -676,7 +679,7 @@
         V((1024, 1), F32),
         V((1024, W), BF),
         V((8, 128, W), BF),
-        V((512, 1408), BF),
+        V((512, 128), BF),
         V((1408, W), BF),
         V((512, W), BF),
         V((512, W), BF),
@@ -685,12 +688,9 @@
         V((8, 128, W), BF),
         V((8, 128, W), BF),
         V((1024, W), BF),
-        V((1024, W), F32),
-        V((1024, W), BF),
-        V((1536, W), F32),
-        V((1024, W), BF),
-        V((256, W), F32),
-        V((256, W), F32),
+        V((4096, W), F32),
+        V((1024, W), BF),
+        V((1024, W), BF),
         V((16, 32, W), BF),
         V((16, 32, W), BF),
         pltpu.SemaphoreType.DMA((256,)),
@@ -700,11 +700,9 @@
     ]
     for _ in range(3):
         scratch += [V((2, YS, 128, W), BF), V((YS, 128, W), BF), V((YS, 128, W), BF), V((YS, 128, W), BF)]
-    for rows in (48, 32):
+    for rows in (48, 32, 32):
         scratch += [V((2, DOM, rows, W), BF), V((DOM, rows, W), BF), V((DOM, rows, W), BF),
                     V((DOM, rows, W), BF), V((YS, rows, W), BF), V((2, DOM, rows, W), BF)]
-    scratch += [V((GRP, 32, W), BF), V((GRP, 32, W), BF), V((DOM, 32, W), BF), V((GRP, 32, W), BF),
-                V((DOM, 48, W), BF), V((DOM, 48, W), BF), V((GRP, 48, W), BF), V((DOM, 48, W), BF)]
     shape = jax.ShapeDtypeStruct
     fine_out, node_grad, edge_grad, grads = pl.pallas_call(
         kernel,
@@ -714,7 +712,7 @@
         out_specs=(hbm,) * 4,
         scratch_shapes=scratch,
         compiler_params=pltpu.CompilerParams(
-            collective_id=0, has_side_effects=True, vmem_limit_bytes=62 * 1024 * 1024
+            collective_id=0, has_side_effects=True, vmem_limit_bytes=64 * 1024 * 1024 - 65536
         ),
     )(
         nodes, edges, senders.reshape(32, 128), receivers.reshape(32, 128), edge_count,

time: 112 us -> 101 us (0.902)
  Pallas kernels: 110 us -> 98.9 us
    pallas_call x1, Pallas kernels: 106 us -> 94.2 us  [body(): pl.pallas_call(kernel, out_shape=(shape((1024, W), BF), shape((1024, W),...]
where the time goes in v3:
time: 101 us; the launch traced here: 100 us
  Pallas kernels  98.9 us (98%)
  between operations  1.45 us (1%)
    pallas_call x1, Pallas kernels, body(): pl.pallas_call(kernel, out_shape=(shape((1024, W), BF), shape((1024, W),...  94.2 us
    pallas_call x1, Pallas kernels, body(): pl.pallas_call(place, out_shape=(shape((1024, W), BF), shape((1024, W), B...  4.72 us

profile of v3, /device:TPU:1, one launch (start us, length us, event | category | flops | bytes accessed | tf_op | source)
XLA Modules:
  0.0 100.4 jit_solution(5774804049074471607)
XLA Ops:
  1.3 94.2 %shard_map.164 = (bf16[1024,256]{1,0:T(8,128)(2,1)}, bf16[1024,256]{1,0:T(8,128)(2,1)}, bf16[4096,256]{1,0:T(8,128)(2,1)}, bf16[3584,256]{1,0:T(8,128)(2,1)}) custom-call(bf16[1024,256]{1,0:T(8,128)(2,1)} %nodes_h.1, bf16[4096,256]{1,0:T(8,128)(2,1)} %edges_h.1, s32[32,128]{1,0:T(8,128)} %bitcast.6, s32[32,128]{1,0:T(8,128)} %bitcast.7, s32[1]{0:T(128)S(6)} %copy.18.cnt, ...), custom_call_target="tpu_custom_call" | custom-call | tf_op jit(solution)/shard_map/pallas_call | solution.py:707
  95.5 4.7 %shard_map.165 = (bf16[1024,256]{1,0:T(8,128)(2,1)}, bf16[1024,256]{1,0:T(8,128)(2,1)}, bf16[4096,256]{1,0:T(8,128)(2,1)}, f32[1792,256]{1,0:T(8,128)}, f32[1792,256]{1,0:T(8,128)}) custom-call(bf16[1024,256]{1,0:T(8,128)(2,1)} %get-tuple-element.9.fine_h, bf16[1024,256]{1,0:T(8,128)(2,1)} %get-tuple-element.10.node_h, ...), custom_call_target="tpu_custom_call" | custom-call | tf_op jit(solution)/shard_map/pallas_call | solution.py:723

commit v4 on v3

--- a/solution.py
+++ b/solution.py
@@ -130,11 +130,8 @@
             act(self.copy(k))
             return carry
 
-        if self.count <= DOM:
-            for k in range(1, self.count):
-                step(k, 0)
-        else:
-            lax.fori_loop(1, self.count, step, 0)
+        for k in sorted(range(1, self.count), key=lambda k: abs(k - self.count // 2)):
+            step(k, 0)
 
     def start(self):
         self.each(lambda c: c.start())
@@ -484,7 +481,6 @@
     sender_sum(core)
     s_cr = mm(cback, cdh).astype(BF)
     sen.pair()
-    x_cout.start()
     put(early.s, halves, 0, mm_tn(ce[...], cdh))
     put(early.s, halves, 256, mm_tn(cact[...], cdz))
     put(early.s, halves, 512, mm_tn(cin, cndh))
@@ -500,14 +496,11 @@
     put(early.s, halves, 1280, mm_tn(cin, s_tot))
     early.stage0()
 
-    x_cout.wait_recv()
-    fine_out[...] = (refined[...].astype(F32) + mm(m_t[...].reshape(1024, 1024), coutb[...].reshape(1024, W))).astype(BF)
-    st_fine = pltpu.make_async_copy(fine_out, fine_out_h, osem.at[0])
-    st_fine.start()
     early.stage1()
     turn(edges, 2048, 8)
     turn(act, 0, 16)
     x_dcin.wait_recv()
+    x_cout.start()
     rg[...] = (cot[...].astype(F32) + 0.125 * mm(m_t[...].reshape(1024, 1024), dcinb[...].reshape(1024, W))).astype(BF)
 
     dz = norm_back(rg[...].astype(F32), yn[...].astype(F32), rsn[...])
@@ -568,6 +561,10 @@
         edge_grad[rows, :] = mm_nt(gpr[rows, :], fw[0:256]).astype(BF)
     st_edge = pltpu.make_async_copy(edge_grad, edge_grad_h, osem.at[1])
     st_edge.start()
+    x_cout.wait_recv()
+    fine_out[...] = (refined[...].astype(F32) + mm(m_t[...].reshape(1024, 1024), coutb[...].reshape(1024, W))).astype(BF)
+    st_fine = pltpu.make_async_copy(fine_out, fine_out_h, osem.at[0])
+    st_fine.start()
     own = dnp[...] + mm_nt(ss[0:1024], fw[256:512]) + mm_nt(s_r[...], fw[512:768])
     late.stage2()
     middle.stage3()

time: 101 us -> 96.7 us (0.957)
  Pallas kernels: 98.9 us -> 95 us
    pallas_call x1, Pallas kernels: 94.2 us -> 90.2 us  [body(): pl.pallas_call(kernel, out_shape=(shape((1024, W), BF), shape((1024, W),...]
where the time goes in v4:
time: 96.7 us; the launch traced here: 96.4 us
  Pallas kernels  95 us (98%)
  between operations  1.45 us (1%)
    pallas_call x1, Pallas kernels, body(): pl.pallas_call(kernel, out_shape=(shape((1024, W), BF), shape((1024, W),...  90.2 us
    pallas_call x1, Pallas kernels, body(): pl.pallas_call(place, out_shape=(shape((1024, W), BF), shape((1024, W), B...  4.72 us

profile of v4, /device:TPU:1, one launch (start us, length us, event | category | flops | bytes accessed | tf_op | source)
XLA Modules:
  0.0 96.4 jit_solution(12028277172112525711)
XLA Ops:
  1.3 90.2 %shard_map.164 = (bf16[1024,256]{1,0:T(8,128)(2,1)}, bf16[1024,256]{1,0:T(8,128)(2,1)}, bf16[4096,256]{1,0:T(8,128)(2,1)}, bf16[3584,256]{1,0:T(8,128)(2,1)}) custom-call(bf16[1024,256]{1,0:T(8,128)(2,1)} %nodes_h.1, bf16[4096,256]{1,0:T(8,128)(2,1)} %edges_h.1, s32[32,128]{1,0:T(8,128)} %bitcast.6, s32[32,128]{1,0:T(8,128)} %bitcast.7, s32[1]{0:T(128)S(6)} %copy.18.cnt, ...), custom_call_target="tpu_custom_call" | custom-call | tf_op jit(solution)/shard_map/pallas_call | solution.py:704
  91.5 4.7 %shard_map.165 = (bf16[1024,256]{1,0:T(8,128)(2,1)}, bf16[1024,256]{1,0:T(8,128)(2,1)}, bf16[4096,256]{1,0:T(8,128)(2,1)}, f32[1792,256]{1,0:T(8,128)}, f32[1792,256]{1,0:T(8,128)}) custom-call(bf16[1024,256]{1,0:T(8,128)(2,1)} %get-tuple-element.9.fine_h, bf16[1024,256]{1,0:T(8,128)(2,1)} %get-tuple-element.10.node_h, ...), custom_call_target="tpu_custom_call" | custom-call | tf_op jit(solution)/shard_map/pallas_call | solution.py:720

commit v5 on v4

--- a/solution.py
+++ b/solution.py
@@ -153,13 +153,25 @@
 class GroupSum:
     def __init__(self, links, s, m, t, r):
         self.links, self.s, self.m, self.t, self.r = links, s, m, t, r
-        self.first = links.exchange("mate", lambda p: s.at[p], lambda k: m)
+        self.order = [2, 1, 3, 0]
+        self.first = {}
+        for k in self.order:
+            q = lax.rem(links.y + k, YS)
+            self.first[k] = links.exchange("mate", lambda p, q=q: s.at[p, q], lambda i, q=q: m.at[q])
         self.second = links.exchange("y", lambda p: t.at[p], lambda k: r.at[k])
 
+    def start(self):
+        for k in self.order:
+            self.first[k].start()
+
     def pair(self):
-        self.first.wait_recv()
-        self.t[...] = (self.s[self.links.core].astype(F32) + self.m[...].astype(F32)).astype(BF)
-        self.second.start()
+        y, core = self.links.y, self.links.core
+        for k in self.order:
+            self.first[k].wait_recv()
+            q = lax.rem(y + k, YS)
+            self.t[q] = (self.s[core, q].astype(F32) + self.m[q].astype(F32)).astype(BF)
+            if k > 0:
+                self.second.copy(k).start()
 
     def result(self):
         self.second.wait_recv()
@@ -332,7 +344,7 @@
     ld_cot.wait()
     for h in range(2):
         pro.s[h] = mm(m_t[h], cot[...]).astype(BF).reshape(YS, 128, W)
-    pro.first.start()
+    pro.start()
 
     ld_fw.wait()
     wcat[0:256] = fw[0:256]
@@ -402,7 +414,7 @@
     hin_t[0:512] = hin[...].reshape(512, W)
 
     res.s[1 - core] = (mm(m_t[1 - core], refined[...]) * 0.125).astype(BF).reshape(YS, 128, W)
-    res.first.start()
+    res.start()
     res.s[core] = (mm(m_t[core], refined[...]) * 0.125).astype(BF).reshape(YS, 128, W)
     res.pair()
 
@@ -477,7 +489,7 @@
         sen.s[half] = mm(jnp.concatenate(blocks, axis=0), cdh).astype(BF).reshape(YS, 128, W)
 
     sender_sum(1 - core)
-    sen.first.start()
+    sen.start()
     sender_sum(core)
     s_cr = mm(cback, cdh).astype(BF)
     sen.pair()
@@ -619,24 +631,24 @@
     moves = [pltpu.make_async_copy(b, c, ssem.at[i]) for i, (a, b, c) in enumerate(parts) if i > 0]
     for c in loads:
         c.start()
+    loads[0].wait()
+
+    def scaled(at, rows, scale):
+        return grads[at:at + rows].astype(F32) * scale
+
+    last = [pltpu.make_async_copy(cwg, cw_o, ssem.at[5]), pltpu.make_async_copy(fwg, fw_o, ssem.at[6])]
+    cwg[0:256] = scaled(0, 256, COARSE_SCALE)
+    cwg[256:768] = scaled(1280, 512, COARSE_SCALE)
+    cwg[768:1792] = scaled(256, 1024, COARSE_SCALE)
+    last[0].start()
     for c, m in zip(loads[1:], moves):
         c.wait()
         m.start()
-    loads[0].wait()
-
-    def scaled(at, rows, scale):
-        return grads[at:at + rows].astype(F32) * scale
-
-    cwg[0:256] = scaled(0, 256, COARSE_SCALE)
-    cwg[256:768] = scaled(1280, 512, COARSE_SCALE)
-    cwg[768:1792] = scaled(256, 1024, COARSE_SCALE)
     fwg[0:256] = scaled(2560, 256, FINE_SCALE)
     fwg[256:768] = scaled(3072, 512, FINE_SCALE)
     fwg[768:1024] = scaled(2816, 256, FINE_SCALE)
     fwg[1024:1792] = scaled(1792, 768, FINE_SCALE)
-    last = [pltpu.make_async_copy(fwg, fw_o, ssem.at[5]), pltpu.make_async_copy(cwg, cw_o, ssem.at[6])]
-    for c in last:
-        c.start()
+    last[1].start()
     for c in moves + last:
         c.wait()
 

time: 96.7 us -> 96.1 us (level)
  no operation moved by 1% of the time
where the time goes in v5:
time: 96.1 us; the launch traced here: 95.8 us
  Pallas kernels  94.4 us (98%)
  between operations  1.45 us (2%)
    pallas_call x1, Pallas kernels, body(): pl.pallas_call(kernel, out_shape=(shape((1024, W), BF), shape((1024, W),...  89.8 us
    pallas_call x1, Pallas kernels, body(): pl.pallas_call(place, out_shape=(shape((1024, W), BF), shape((1024, W), B...  4.59 us

profile of v5, /device:TPU:1, one launch (start us, length us, event | category | flops | bytes accessed | tf_op | source)
XLA Modules:
  0.0 95.8 jit_solution(10309401843544483638)
XLA Ops:
  1.3 89.8 %shard_map.164 = (bf16[1024,256]{1,0:T(8,128)(2,1)}, bf16[1024,256]{1,0:T(8,128)(2,1)}, bf16[4096,256]{1,0:T(8,128)(2,1)}, bf16[3584,256]{1,0:T(8,128)(2,1)}) custom-call(bf16[1024,256]{1,0:T(8,128)(2,1)} %nodes_h.1, bf16[4096,256]{1,0:T(8,128)(2,1)} %edges_h.1, s32[32,128]{1,0:T(8,128)} %bitcast.6, s32[32,128]{1,0:T(8,128)} %bitcast.7, s32[1]{0:T(128)S(6)} %copy.18.cnt, ...), custom_call_target="tpu_custom_call" | custom-call | tf_op jit(solution)/shard_map/pallas_call | solution.py:716
  91.1 4.6 %shard_map.165 = (bf16[1024,256]{1,0:T(8,128)(2,1)}, bf16[1024,256]{1,0:T(8,128)(2,1)}, bf16[4096,256]{1,0:T(8,128)(2,1)}, f32[1792,256]{1,0:T(8,128)}, f32[1792,256]{1,0:T(8,128)}) custom-call(bf16[1024,256]{1,0:T(8,128)(2,1)} %get-tuple-element.9.fine_h, bf16[1024,256]{1,0:T(8,128)(2,1)} %get-tuple-element.10.node_h, ...), custom_call_target="tpu_custom_call" | custom-call | tf_op jit(solution)/shard_map/pallas_call | solution.py:732

commit v6 on v4

--- a/solution.py
+++ b/solution.py
@@ -354,15 +354,15 @@
     ld_edges.wait()
 
     def edge_local(i, c):
-        rows = pl.ds(pl.multiple_of(i * BIG, BIG), BIG)
-        tiles = [i * (BIG // 512) + q for q in range(BIG // 512)]
+        rows = pl.ds(0, 4096)
+        tiles = range(TILES)
         far = [jnp.concatenate([oh[t, b] for b in range(8)], axis=1) for t in tiles]
         near = [mm(ohr[t], p_r[pl.ds(pl.multiple_of(t * 128, 128), 128), :]) for t in tiles]
         joined = jnp.concatenate([edges[rows, :], jnp.concatenate(far, axis=0)], axis=1)
         work[rows, :] = mm(joined, wcat[0:1280]) + jnp.concatenate(near, axis=0)
         return c
 
-    lax.fori_loop(0, 4096 // BIG, edge_local, 0)
+    edge_local(0, 0)
     x_halo.wait_recv()
     wcat[1280:1792] = mm(hin[...].reshape(512, W), fw[256:512]).astype(BF)
 

time: 96.7 us -> 96.4 us (level)
  no operation moved by 1% of the time
where the time goes in v6:
time: 96.4 us; the launch traced here: 96.2 us
  Pallas kernels  94.7 us (98%)
  between operations  1.45 us (2%)
    pallas_call x1, Pallas kernels, body(): pl.pallas_call(kernel, out_shape=(shape((1024, W), BF), shape((1024, W),...  90 us
    pallas_call x1, Pallas kernels, body(): pl.pallas_call(place, out_shape=(shape((1024, W), BF), shape((1024, W), B...  4.72 us

profile of v6, /device:TPU:1, one launch (start us, length us, event | category | flops | bytes accessed | tf_op | source)
XLA Modules:
  0.0 96.2 jit_solution(16396069961188471163)
XLA Ops:
  1.3 90.0 %shard_map.164 = (bf16[1024,256]{1,0:T(8,128)(2,1)}, bf16[1024,256]{1,0:T(8,128)(2,1)}, bf16[4096,256]{1,0:T(8,128)(2,1)}, bf16[3584,256]{1,0:T(8,128)(2,1)}) custom-call(bf16[1024,256]{1,0:T(8,128)(2,1)} %nodes_h.1, bf16[4096,256]{1,0:T(8,128)(2,1)} %edges_h.1, s32[32,128]{1,0:T(8,128)} %bitcast.6, s32[32,128]{1,0:T(8,128)} %bitcast.7, s32[1]{0:T(128)S(6)} %copy.18.cnt, ...), custom_call_target="tpu_custom_call" | custom-call | tf_op jit(solution)/shard_map/pallas_call | solution.py:704
  91.3 4.7 %shard_map.165 = (bf16[1024,256]{1,0:T(8,128)(2,1)}, bf16[1024,256]{1,0:T(8,128)(2,1)}, bf16[4096,256]{1,0:T(8,128)(2,1)}, f32[1792,256]{1,0:T(8,128)}, f32[1792,256]{1,0:T(8,128)}) custom-call(bf16[1024,256]{1,0:T(8,128)(2,1)} %get-tuple-element.9.fine_h, bf16[1024,256]{1,0:T(8,128)(2,1)} %get-tuple-element.10.node_h, ...), custom_call_target="tpu_custom_call" | custom-call | tf_op jit(solution)/shard_map/pallas_call | solution.py:720
